TPU v7x, 32 devices: a whole 2x2x4 slice. The times are simulated.
32 devices in a mesh: expert: 16 (over z, y, x), dp: 2 (over core).
Axes of the slice: x: 2, y: 2, z: 4, core: 2. Of those that a mesh axis runs over, the one named last changes fastest.
Arguments:
- tokens: bfloat16 [4096, 2048], P(('expert', 'dp')), may hold values from -6 to 6
- out_grad: bfloat16 [4096, 2048], P(('expert', 'dp')), may hold values from -6 to 6
- expert_ids: int32 [4096, 8], P(('expert', 'dp')), may hold values from 0 to 15, all different within a row; in each aligned block of 128 rows (0 to 127, 128 to 255, ...) at most 72 rows name the same one
- route_scores: float32 [4096, 8], P(('expert', 'dp')), may hold values from 0.05 to 1
- old_slot: int32 [16], replicated, may hold values from 0 to 15, as said below
- new_slot: int32 [16], replicated, may hold values from 0 to 15, as said below
- gate_up: bfloat16 [16, 2048, 768], P('expert'), may hold values from -0.125 to 0.125
- down: bfloat16 [16, 384, 2048], P('expert'), may hold values from -0.3125 to 0.3125
- first_gu: bfloat16 [16, 2048, 768], P('expert', 'dp'), may hold values from -12 to 12
- second_gu: bfloat16 [16, 2048, 768], P('expert', 'dp'), may hold values from 4 to 64
- first_down: bfloat16 [16, 384, 2048], P('expert', None, 'dp'), may hold values from -6 to 6
- second_down: bfloat16 [16, 384, 2048], P('expert', None, 'dp'), may hold values from 1 to 16
Outputs:
- mixed: bfloat16 [4096, 2048], P(('expert', 'dp'))
- token_grad: bfloat16 [4096, 2048], P(('expert', 'dp'))
- update_gu: bfloat16 [16, 2048, 768], P('expert', 'dp')
- update_down: bfloat16 [16, 384, 2048], P('expert', None, 'dp')
Inputs may be any that keep to these rules, and one draw needn't show every extreme that they name: `expert_ids`: each row names 8 different experts; among the rows of one device no expert is named more than 72 times. `old_slot`: A permutation of the slots. `new_slot`: A permutation of the slots; it differs from old_slot in exactly 8 experts.
All inputs are finite; a program needn't handle non-finite values.
Results may differ from a plain program's by a relative error of at most 0.012.
Values may be sent and summed in bfloat16 or wider, within the bound.
A program may use at most 192 MiB of HBM per device.

v0:
```python
import jax
import jax.numpy as jnp
from jax import lax
from jax.sharding import PartitionSpec as P

beta_one = 0.9
beta_two = 0.95
epsilon = 1e-08


def as_sent(array):
    return jax.tree.map(lambda a: a.astype(jnp.bfloat16) if a.dtype == jnp.float32 else a, array)


def expert_forward(rows_x, w_gu, w_down):
    hidden = w_down.shape[0]
    both = jnp.dot(rows_x, w_gu, preferred_element_type=jnp.float32)
    gate = both[:, :hidden]
    upper = both[:, hidden:]
    activated = (gate * jax.nn.sigmoid(gate) * upper).astype(jnp.bfloat16)
    output = jnp.dot(activated, w_down, preferred_element_type=jnp.float32).astype(jnp.bfloat16)
    return (both, activated, output)


def expert_backward(rows_x, rows_cot, both, activated, w_gu, w_down):
    hidden = w_down.shape[0]
    gate = both[:, :hidden]
    upper = both[:, hidden:]
    sigmoid_gate = jax.nn.sigmoid(gate)
    grad_act = lax.dot_general(
        rows_cot, w_down, (((1,), (1,)), ((), ())), preferred_element_type=jnp.float32
    )
    grad_gate = grad_act * upper * (sigmoid_gate * (1.0 + gate * (1.0 - sigmoid_gate)))
    grad_upper = grad_act * gate * sigmoid_gate
    grad_both = jnp.concatenate([grad_gate, grad_upper], axis=1).astype(jnp.bfloat16)
    row_grad = lax.dot_general(
        grad_both, w_gu, (((1,), (1,)), ((), ())), preferred_element_type=jnp.float32
    ).astype(jnp.bfloat16)
    grad_gu = lax.dot_general(
        rows_x, grad_both, (((0,), (0,)), ((), ())), preferred_element_type=jnp.float32
    )
    grad_down = lax.dot_general(
        activated, rows_cot, (((0,), (0,)), ((), ())), preferred_element_type=jnp.float32
    )
    return (row_grad, grad_gu, grad_down)


def adam_direction(first, second, grad):
    first_new = beta_one * first.astype(jnp.float32) + (1.0 - beta_one) * grad
    second_new = beta_two * second.astype(jnp.float32) + (1.0 - beta_two) * grad * grad
    first_fix = 1.0 - beta_one**10.0
    second_fix = 1.0 - beta_two**10.0
    return (first_new / first_fix / (jnp.sqrt(second_new / second_fix) + epsilon)).astype(
        jnp.bfloat16
    )


def relocate(blocks, source, count):
    flats = tuple((block.reshape(count, -1) for block in blocks))
    spread = jax.tree.map(
        lambda part, own: part.astype(own.dtype),
        lax.all_to_all(as_sent(flats), "expert", split_axis=0, concat_axis=0, tiled=True),
        flats,
    )
    ordered = tuple((jnp.take(piece, source, axis=0) for piece in spread))
    landed = jax.tree.map(
        lambda part, own: part.astype(own.dtype),
        lax.all_to_all(as_sent(ordered), "expert", split_axis=0, concat_axis=0, tiled=True),
        ordered,
    )
    return tuple((piece.reshape(block.shape) for piece, block in zip(landed, blocks)))


def per_device(
    tokens,
    out_grad,
    expert_ids,
    route_scores,
    old_slot,
    new_slot,
    gate_up,
    down,
    first_gu,
    second_gu,
    first_down,
    second_down,
):
    count = lax.axis_size("expert")
    tok_rows, width = tokens.shape
    top = expert_ids.shape[1]
    capacity = max(2, tok_rows * top * 9 // (8 * count))
    rows = count * capacity
    lanes = jnp.arange(count, dtype=jnp.int32)
    owner = new_slot[None, :] == lanes[:, None]
    source = jnp.sum(jnp.where(owner, old_slot[None, :], 0), axis=1)
    moments = (first_gu, second_gu, first_down, second_down)
    moved = relocate((gate_up, down) + moments, source, count)
    state = moved[2:]
    w_gu = moved[0][0]
    w_down = moved[1][0]
    probs = route_scores / jnp.sum(route_scores, axis=1, keepdims=True)
    target = jnp.sum(
        jnp.where(expert_ids[:, :, None] == lanes[None, None, :], new_slot[None, None, :], 0),
        axis=2,
    )
    flat_target = target.reshape(-1)
    onehot = (flat_target[:, None] == lanes[None, :]).astype(jnp.int32)
    place = jnp.sum(onehot * (jnp.cumsum(onehot, axis=0) - 1), axis=1)
    slot = flat_target * capacity + place
    match = slot[None, :] == jnp.arange(rows, dtype=jnp.int32)[:, None]
    pick = jnp.any(match.reshape(rows, tok_rows, top), axis=2).astype(jnp.bfloat16)
    slot_prob = jnp.sum(jnp.where(match, probs.reshape(1, -1), 0.0), axis=1)
    send_x = (
        jnp.dot(pick, tokens, preferred_element_type=jnp.float32)
        .astype(jnp.bfloat16)
        .reshape(count, capacity, width)
    )
    send_cot = (
        (jnp.dot(pick, out_grad, preferred_element_type=jnp.float32) * slot_prob[:, None])
        .astype(jnp.bfloat16)
        .reshape(count, capacity, width)
    )
    recv_x = lax.all_to_all(send_x, "expert", split_axis=0, concat_axis=0, tiled=True)
    rows_x = recv_x.reshape(rows, width)
    both, activated, output = expert_forward(rows_x, w_gu, w_down)
    back_out = lax.all_to_all(
        output.reshape(count, capacity, width), "expert", split_axis=0, concat_axis=0, tiled=True
    )
    recv_cot = lax.all_to_all(send_cot, "expert", split_axis=0, concat_axis=0, tiled=True)
    rows_cot = recv_cot.reshape(rows, width)
    row_grad, grad_gu, grad_down = expert_backward(rows_x, rows_cot, both, activated, w_gu, w_down)
    back_grad = lax.all_to_all(
        row_grad.reshape(count, capacity, width), "expert", split_axis=0, concat_axis=0, tiled=True
    )
    got_out = jnp.take(back_out.reshape(rows, width), slot, axis=0).reshape(tok_rows, top, width)
    got_grad = jnp.take(back_grad.reshape(rows, width), slot, axis=0).reshape(tok_rows, top, width)
    mixed = jnp.sum(probs[:, :, None] * got_out.astype(jnp.float32), axis=1).astype(jnp.bfloat16)
    token_grad = jnp.sum(got_grad.astype(jnp.float32), axis=1).astype(jnp.bfloat16)
    share_gu, share_down = (
        lax.psum_scatter(
            grad_gu.astype(jnp.bfloat16), "dp", scatter_dimension=0, tiled=True
        ).astype(jnp.float32),
        lax.psum_scatter(
            grad_down.astype(jnp.bfloat16), "dp", scatter_dimension=1, tiled=True
        ).astype(jnp.float32),
    )
    update_gu = adam_direction(state[0][0], state[1][0], share_gu)[None]
    update_down = adam_direction(state[2][0], state[3][0], share_down)[None]
    return (mixed, token_grad, update_gu, update_down)


def solution(mesh):
    placed = (
        P(("expert", "dp"), None),
        P(("expert", "dp"), None),
        P(("expert", "dp"), None),
        P(("expert", "dp"), None),
        P(),
        P(),
        P("expert", None, None),
        P("expert", None, None),
        P("expert", "dp", None),
        P("expert", "dp", None),
        P("expert", None, "dp"),
        P("expert", None, "dp"),
    )
    return jax.shard_map(
        per_device,
        mesh=mesh,
        in_specs=placed,
        out_specs=(
            P(("expert", "dp"), None),
            P(("expert", "dp"), None),
            P("expert", "dp", None),
            P("expert", None, "dp"),
        ),
        check_vma=False,
    )
```

profile of v0, /device:TPU:0, one launch (start us, length us, event | category | flops | bytes accessed | tf_op | source)
XLA Modules:
  0.0 1052.3 jit_solution(9777426787139680111)
XLA Ops:
  11.9 5.4 reduce.19
  18.7 8.7 all-to-all-start.12
  31.5 5.4 reduce.20
  38.4 8.8 all-to-all-done.12
  47.2 5.4 all-to-all-start.14
  56.1 11.8 %reduce.13 = bf16[16,49152]{1,0:T(8,128)(2,1)S(1)} reduce(bf16[16,1,49152]{2,1,0:T(2,128)(2,1)} %all_to_all.129, bf16[]{:T(256)} %broadcast.198), dimensions={1}, to_apply=%all_to_all.129.reduce_sub_computation | reduce | bytes 3145730 | tf_op jit(solution)/shard_map/all_to_all | solution.py:62
  71.2 6.2 all-to-all-start.8
  80.9 11.8 %reduce.14 = bf16[16,49152]{1,0:T(8,128)(2,1)S(1)} reduce(bf16[16,1,49152]{2,1,0:T(2,128)(2,1)} %all_to_all.130, bf16[]{:T(256)} %broadcast.198), dimensions={1}, to_apply=%all_to_all.130.reduce_sub_computation | reduce | bytes 3145730 | tf_op jit(solution)/shard_map/all_to_all | solution.py:62
  94.8 15.3 %all-to-all-done.8 = bf16[16,2,24576]{2,1,0:T(2,128)(2,1)} async-done(((bf16[16,2,24576]{2,1,0:T(2,128)(2,1)}), bf16[16,2,24576]{2,1,0:T(2,128)(2,1)}, u32[]{:S(2)}, u32[]{:S(2)}) %all-to-all-start.8) | async-done | bytes 1572896 | tf_op jit(solution)/shard_map/all_to_all | solution.py:62
  110.1 7.8 all-to-all-start.10
  117.9 4.6 all_to_all.128
  122.5 11.8 %reduce.15 = bf16[16,49152]{1,0:T(8,128)(2,1)S(1)} reduce(bf16[16,1,49152]{2,1,0:T(2,128)(2,1)} %all_to_all.128, bf16[]{:T(256)} %broadcast.198), dimensions={1}, to_apply=%all_to_all.128.reduce_sub_computation | reduce | bytes 3145730 | tf_op jit(solution)/shard_map/all_to_all | solution.py:62
  141.8 5.2 reshape.314
  152.4 7.0 all-to-all-start.3
  165.7 26.7 %all-to-all-done.3 = bf16[16,2,24576]{2,1,0:T(2,128)(2,1)S(1)} async-done(((bf16[16,2,24576]{2,1,0:T(2,128)(2,1)}), bf16[16,2,24576]{2,1,0:T(2,128)(2,1)S(1)}, u32[]{:S(2)}, u32[]{:S(2)}) %all-to-all-start.3) | async-done | bytes 1572896 | tf_op jit(solution)/shard_map/all_to_all | solution.py:62
  192.4 7.5 all-to-all-start.13
  203.8 10.0 reshape.310
  220.1 10.0 reshape.306
  236.5 10.0 reshape.302
  252.8 7.0 all-to-all-start.15
  271.6 6.8 all-to-all-done.15
  278.4 5.0 all-to-all-start.4
  283.4 10.7 %all_to_all.127 = bf16[16,1,98304]{2,1,0:T(2,128)(2,1)} reshape(bf16[1,2048,768]{2,1,0:T(8,128)(2,1)} %param.24) | data formatting | bytes 6291456 | tf_op jit(solution)/shard_map/all_to_all | solution.py:62
  294.1 20.8 %reduce.11 = bf16[16,98304]{1,0:T(8,128)(2,1)} reduce(bf16[16,1,98304]{2,1,0:T(2,128)(2,1)} %all_to_all.127, bf16[]{:T(256)} %broadcast.198), dimensions={1}, to_apply=%all_to_all.127.reduce_sub_computation | reduce | bytes 6291458 | tf_op jit(solution)/shard_map/all_to_all | solution.py:62
  314.9 5.3 reshape.297
  320.2 7.0 all-to-all-start.1
  333.1 54.0 %all-to-all-done.1 = bf16[16,2,49152]{2,1,0:T(2,128)(2,1)} async-done(((bf16[16,2,49152]{2,1,0:T(2,128)(2,1)}), bf16[16,2,49152]{2,1,0:T(2,128)(2,1)}, u32[]{:S(2)}, u32[]{:S(2)}) %all-to-all-start.1) | async-done | bytes 3145760 | tf_op jit(solution)/shard_map/all_to_all | solution.py:62
  387.1 14.0 %all-to-all-start.9 = ((bf16[16,2,24576]{2,1,0:T(2,128)(2,1)}), bf16[16,2,24576]{2,1,0:T(2,128)(2,1)S(1)}, u32[]{:S(2)}, u32[]{:S(2)}) async-start(bf16[16,2,24576]{2,1,0:T(2,128)(2,1)} %reshape.311), calls=%async_computation.9 | async-start | bytes 3145728 | tf_op jit(solution)/shard_map/all_to_all | solution.py:68
  401.4 4.5 reduce-window.6
  414.3 20.3 %all-to-all-done.9 = bf16[16,2,24576]{2,1,0:T(2,128)(2,1)S(1)} async-done(((bf16[16,2,24576]{2,1,0:T(2,128)(2,1)}), bf16[16,2,24576]{2,1,0:T(2,128)(2,1)S(1)}, u32[]{:S(2)}, u32[]{:S(2)}) %all-to-all-start.9) | async-done | bytes 1572896 | tf_op jit(solution)/shard_map/all_to_all | solution.py:68
  435.9 7.8 all-to-all-start
  448.0 11.5 %reshape.298 = bf16[16,1,98304]{2,1,0:T(2,128)(2,1)} reshape(bf16[16,2,49152]{2,1,0:T(2,128)(2,1)} %all-to-all-done.1) | data formatting | bytes 6291456
  459.4 6.2 copy.86
  470.0 61.2 %all-to-all-done = bf16[16,72,2048]{2,1,0:T(8,128)(2,1)} async-done(((bf16[16,72,2048]{2,1,0:T(8,128)(2,1)}), bf16[16,72,2048]{2,1,0:T(8,128)(2,1)}, u32[]{:S(2)}, u32[]{:S(2)}) %all-to-all-start) | async-done | bytes 4718624 | tf_op jit(solution)/shard_map/all_to_all | solution.py:123
  531.2 21.7 %all-to-all-start.6 = ((bf16[16,72,2048]{2,1,0:T(8,128)(2,1)}), bf16[16,72,2048]{2,1,0:T(8,128)(2,1)}, u32[]{:S(2)}, u32[]{:S(2)}) async-start(bf16[16,72,2048]{2,1,0:T(8,128)(2,1)} %bitcast.86), calls=%async_computation.6 | async-start | bytes 9437184 | tf_op jit(solution)/shard_map/all_to_all | solution.py:129
  558.9 5.3 reshape.299
  564.2 76.1 %all-to-all-done.6 = bf16[16,72,2048]{2,1,0:T(8,128)(2,1)} async-done(((bf16[16,72,2048]{2,1,0:T(8,128)(2,1)}), bf16[16,72,2048]{2,1,0:T(8,128)(2,1)}, u32[]{:S(2)}, u32[]{:S(2)}) %all-to-all-start.6) | async-done | bytes 4718624 | tf_op jit(solution)/shard_map/all_to_all | solution.py:129
  640.3 21.3 %all-to-all-start.2 = ((bf16[16,2,49152]{2,1,0:T(2,128)(2,1)}), bf16[16,2,49152]{2,1,0:T(2,128)(2,1)S(1)}, u32[]{:S(2)}, u32[]{:S(2)}) async-start(bf16[16,2,49152]{2,1,0:T(2,128)(2,1)} %reshape.299), calls=%async_computation.2 | async-start | bytes 6291456 | tf_op jit(solution)/shard_map/all_to_all | solution.py:68
  668.7 53.4 %all-to-all-done.2 = bf16[16,2,49152]{2,1,0:T(2,128)(2,1)S(1)} async-done(((bf16[16,2,49152]{2,1,0:T(2,128)(2,1)}), bf16[16,2,49152]{2,1,0:T(2,128)(2,1)S(1)}, u32[]{:S(2)}, u32[]{:S(2)}) %all-to-all-start.2) | async-done | bytes 3145760 | tf_op jit(solution)/shard_map/all_to_all | solution.py:68
  723.8 14.3 %all-to-all-start.11 = ((bf16[16,2,24576]{2,1,0:T(2,128)(2,1)}), bf16[16,2,24576]{2,1,0:T(2,128)(2,1)}, u32[]{:S(2)}, u32[]{:S(2)}) async-start(bf16[16,2,24576]{2,1,0:T(2,128)(2,1)} %reshape.307), calls=%async_computation.12 | async-start | bytes 3145728 | tf_op jit(solution)/shard_map/all_to_all | solution.py:68
  738.1 8.1 reshape.304
  746.2 10.7 %reduce.2 = bf16[16,49152]{1,0:T(8,128)(2,1)} reduce(bf16[16,1,49152]{2,1,0:T(2,128)(2,1)S(1)} %reshape.304, bf16[]{:T(256)} %constant.95), dimensions={1}, to_apply=%all_to_all.103.reduce_sub_computation | reduce | bytes 3145730 | tf_op jit(solution)/shard_map/all_to_all | solution.py:68
  759.9 7.6 reshape.300
  767.5 18.7 %reduce.1 = bf16[16,98304]{1,0:T(8,128)(2,1)S(1)} reduce(bf16[16,1,98304]{2,1,0:T(2,128)(2,1)} %reshape.300, bf16[]{:T(256)} %constant.95), dimensions={1}, to_apply=%all_to_all.98.reduce_sub_computation | reduce | bytes 6291458 | tf_op jit(solution)/shard_map/all_to_all | solution.py:68
  788.8 8.0 fusion.28
  796.9 5.3 multiply_convert_fusion.1
  803.4 5.6 convolution_convert_fusion
  808.9 7.0 all-to-all-start.7
  816.5 5.7 convolution_convert_fusion.4
  826.5 76.9 %all-to-all-done.7 = bf16[16,72,2048]{2,1,0:T(8,128)(2,1)} async-done(((bf16[16,72,2048]{2,1,0:T(8,128)(2,1)}), bf16[16,72,2048]{2,1,0:T(8,128)(2,1)}, u32[]{:S(2)}, u32[]{:S(2)}) %all-to-all-start.7) | async-done | bytes 4718624 | tf_op jit(solution)/shard_map/all_to_all | solution.py:132
  903.4 21.1 %all-to-all-start.5 = ((bf16[16,72,2048]{2,1,0:T(8,128)(2,1)}), bf16[16,72,2048]{2,1,0:T(8,128)(2,1)}, u32[]{:S(2)}, u32[]{:S(2)}) async-start(bf16[16,72,2048]{2,1,0:T(8,128)(2,1)} %bitcast.87), calls=%async_computation.5 | async-start | bytes 9437184 | tf_op jit(solution)/shard_map/all_to_all | solution.py:126
  924.6 9.0 convolution_convert_fusion.3
  938.0 4.9 multiply_reduce_fusion.3
  944.4 4.6 reshape.316
  948.9 4.9 multiply_reduce_fusion.2
  955.3 8.1 reshape.312
  963.4 11.6 %multiply_reduce_fusion.1 = f32[16,49152]{1,0:T(8,128)} fusion(bf16[16,1,49152]{2,1,0:T(2,128)(2,1)S(1)} %reshape.312), kind=kLoop, calls=%fused_computation.33 | loop fusion | flops 1572864 | bytes 4718592 | tf_op jit(solution)/shard_map/mul | solution.py:49
  978.3 8.5 reshape.308
  986.8 11.6 %multiply_reduce_fusion = f32[16,49152]{1,0:T(8,128)} fusion(bf16[16,1,49152]{2,1,0:T(2,128)(2,1)S(1)} %reshape.308), kind=kLoop, calls=%fused_computation.32 | loop fusion | flops 1572864 | bytes 4718592 | tf_op jit(solution)/shard_map/mul | solution.py:50
  1006.1 5.6 fusion.19
  1011.6 11.8 %gather_fusion.3 = bf16[1024,2048]{1,0:T(8,128)(2,1)} fusion(bf16[1152,2048]{1,0:T(8,128)(2,1)} %bitcast.14, s32[1024]{0:T(1024)S(1)} %fusion.24), kind=kCustom, calls=%fused_computation.5.clone | custom fusion | bytes 8392704 | tf_op jit(solution)/shard_map/jit(_take)/gather | solution.py:136
  1023.5 11.8 %gather_fusion.2 = bf16[1024,2048]{1,0:T(8,128)(2,1)} fusion(bf16[1152,2048]{1,0:T(8,128)(2,1)} %bitcast.9, s32[1024]{0:T(1024)S(1)} %fusion.24), kind=kCustom, calls=%fused_computation.1.clone | custom fusion | bytes 8392704 | tf_op jit(solution)/shard_map/jit(_take)/gather | solution.py:135
  1035.2 5.3 bitcast_reduce_fusion
  1040.5 4.7 fusion
  (136 shorter events, 147.1 us)
Async XLA Ops:
  7.2 403.6 %copy-start = (bf16[128,2048]{1,0:T(8,128)(2,1)S(1)}, bf16[128,2048]{1,0:T(8,128)(2,1)}, u32[]{:S(2)}) copy-start(bf16[128,2048]{1,0:T(8,128)(2,1)} %param.18) | copy-start | bytes 1572868
  18.7 28.5 %all-to-all-start.12 = ((bf16[16,2,12288]{2,1,0:T(2,128)(2,1)}), bf16[16,2,12288]{2,1,0:T(2,128)(2,1)}, u32[]{:S(2)}, u32[]{:S(2)}) async-start(bf16[16,2,12288]{2,1,0:T(2,128)(2,1)} %reshape.317), calls=%async_computation.13 | async-start | bytes 1572864 | tf_op jit(solution)/shard_map/all_to_all | solution.py:62
  36.9 15.7 %copy-start.12 = (bf16[1,1024,768]{2,1,0:T(8,128)(2,1)S(1)}, bf16[1,1024,768]{2,1,0:T(8,128)(2,1)}, u32[]{:S(2)}) copy-start(bf16[1,1024,768]{2,1,0:T(8,128)(2,1)} %param.26) | copy-start | bytes 4718596
  47.2 24.0 %all-to-all-start.14 = ((bf16[16,2,12288]{2,1,0:T(2,128)(2,1)}), bf16[16,2,12288]{2,1,0:T(2,128)(2,1)S(1)}, u32[]{:S(2)}, u32[]{:S(2)}) async-start(bf16[16,2,12288]{2,1,0:T(2,128)(2,1)} %reshape.313), calls=%async_computation.16 | async-start | bytes 1572864 | tf_op jit(solution)/shard_map/all_to_all | solution.py:62
  70.0 7.4 copy-start.13
  71.2 9.7 copy-start.10
  71.2 38.9 %all-to-all-start.8 = ((bf16[16,2,24576]{2,1,0:T(2,128)(2,1)}), bf16[16,2,24576]{2,1,0:T(2,128)(2,1)}, u32[]{:S(2)}, u32[]{:S(2)}) async-start(bf16[16,2,24576]{2,1,0:T(2,128)(2,1)} %reshape.309), calls=%async_computation.8 | async-start | bytes 3145728 | tf_op jit(solution)/shard_map/all_to_all | solution.py:62
  94.8 23.1 %copy-start.14 = (bf16[1,384,2048]{2,1,0:T(8,128)(2,1)S(1)}, bf16[1,384,2048]{2,1,0:T(8,128)(2,1)}, u32[]{:S(2)}) copy-start(bf16[1,384,2048]{2,1,0:T(8,128)(2,1)} %param.25) | copy-start | bytes 4718596
  110.1 42.2 %all-to-all-start.10 = ((bf16[16,2,24576]{2,1,0:T(2,128)(2,1)}), bf16[16,2,24576]{2,1,0:T(2,128)(2,1)}, u32[]{:S(2)}, u32[]{:S(2)}) async-start(bf16[16,2,24576]{2,1,0:T(2,128)(2,1)} %reshape.305), calls=%async_computation.11 | async-start | bytes 3145728 | tf_op jit(solution)/shard_map/all_to_all | solution.py:62
  122.5 14.0 %copy-start.18 = (s32[16]{0:T(128)S(1)}, s32[16]{0:T(128)}, u32[]{:S(2)}) copy-start(s32[16]{0:T(128)} %param.23) | copy-start | bytes 196
  122.5 14.0 %copy-start.19 = (s32[16]{0:T(128)S(1)}, s32[16]{0:T(128)}, u32[]{:S(2)}) copy-start(s32[16]{0:T(128)} %param.22) | copy-start | bytes 196
  152.4 40.1 %all-to-all-start.3 = ((bf16[16,2,24576]{2,1,0:T(2,128)(2,1)}), bf16[16,2,24576]{2,1,0:T(2,128)(2,1)S(1)}, u32[]{:S(2)}, u32[]{:S(2)}) async-start(bf16[16,2,24576]{2,1,0:T(2,128)(2,1)} %reshape.301), calls=%async_computation.3 | async-start | bytes 3145728 | tf_op jit(solution)/shard_map/all_to_all | solution.py:62
  192.4 11.4 %copy-start.7 = (bf16[16,2,24576]{2,1,0:T(2,128)(2,1)}, bf16[16,2,24576]{2,1,0:T(2,128)(2,1)S(1)}, u32[]{:S(2)}) copy-start(bf16[16,2,24576]{2,1,0:T(2,128)(2,1)S(1)} %all-to-all-done.3) | copy-start | bytes 4718596
  192.4 60.4 %all-to-all-start.13 = ((bf16[16,2,12288]{2,1,0:T(2,128)(2,1)}), bf16[16,2,12288]{2,1,0:T(2,128)(2,1)}, u32[]{:S(2)}, u32[]{:S(2)}) async-start(bf16[16,2,12288]{2,1,0:T(2,128)(2,1)} %reshape.319), calls=%async_computation.14 | async-start | bytes 1572864 | tf_op jit(solution)/shard_map/all_to_all | solution.py:68
  252.8 25.6 %all-to-all-start.15 = ((bf16[16,2,12288]{2,1,0:T(2,128)(2,1)}), bf16[16,2,12288]{2,1,0:T(2,128)(2,1)S(1)}, u32[]{:S(2)}, u32[]{:S(2)}) async-start(bf16[16,2,12288]{2,1,0:T(2,128)(2,1)} %reshape.315), calls=%async_computation.17 | async-start | bytes 1572864 | tf_op jit(solution)/shard_map/all_to_all | solution.py:68
  278.4 15.7 %copy-start.9 = (bf16[16,2,12288]{2,1,0:T(2,128)(2,1)}, bf16[16,2,12288]{2,1,0:T(2,128)(2,1)S(1)}, u32[]{:S(2)}) copy-start(bf16[16,2,12288]{2,1,0:T(2,128)(2,1)S(1)} %all-to-all-done.15) | copy-start | bytes 2359300
  278.4 41.8 %all-to-all-start.4 = ((bf16[16,2,24576]{2,1,0:T(2,128)(2,1)}), bf16[16,2,24576]{2,1,0:T(2,128)(2,1)}, u32[]{:S(2)}, u32[]{:S(2)}) async-start(bf16[16,2,24576]{2,1,0:T(2,128)(2,1)} %reshape.303), calls=%async_computation.4 | async-start | bytes 3145728 | tf_op jit(solution)/shard_map/all_to_all | solution.py:68
  320.2 66.9 %all-to-all-start.1 = ((bf16[16,2,49152]{2,1,0:T(2,128)(2,1)}), bf16[16,2,49152]{2,1,0:T(2,128)(2,1)}, u32[]{:S(2)}, u32[]{:S(2)}) async-start(bf16[16,2,49152]{2,1,0:T(2,128)(2,1)} %reshape.297), calls=%async_computation.1 | async-start | bytes 6291456 | tf_op jit(solution)/shard_map/all_to_all | solution.py:62
  329.8 71.3 %copy-start.17 = (s32[128,8]{0,1:T(8,128)S(1)}, s32[128,8]{0,1:T(8,128)}, u32[]{:S(2)}) copy-start(s32[128,8]{0,1:T(8,128)} %param.20) | copy-start | bytes 12292
  387.1 47.6 %all-to-all-start.9 = ((bf16[16,2,24576]{2,1,0:T(2,128)(2,1)}), bf16[16,2,24576]{2,1,0:T(2,128)(2,1)S(1)}, u32[]{:S(2)}, u32[]{:S(2)}) async-start(bf16[16,2,24576]{2,1,0:T(2,128)(2,1)} %reshape.311), calls=%async_computation.9 | async-start | bytes 3145728 | tf_op jit(solution)/shard_map/all_to_all | solution.py:68
  434.6 1.2 copy-start.6
  434.6 9.0 copy-start.16
  434.6 9.8 copy-start.15
  435.9 95.3 %all-to-all-start = ((bf16[16,72,2048]{2,1,0:T(8,128)(2,1)}), bf16[16,72,2048]{2,1,0:T(8,128)(2,1)}, u32[]{:S(2)}, u32[]{:S(2)}) async-start(bf16[16,72,2048]{2,1,0:T(8,128)(2,1)} %bitcast.85), calls=%async_computation | async-start | bytes 9437184 | tf_op jit(solution)/shard_map/all_to_all | solution.py:123
  531.2 109.0 %all-to-all-start.6 = ((bf16[16,72,2048]{2,1,0:T(8,128)(2,1)}), bf16[16,72,2048]{2,1,0:T(8,128)(2,1)}, u32[]{:S(2)}, u32[]{:S(2)}) async-start(bf16[16,72,2048]{2,1,0:T(8,128)(2,1)} %bitcast.86), calls=%async_computation.6 | async-start | bytes 9437184 | tf_op jit(solution)/shard_map/all_to_all | solution.py:129
  640.3 81.9 %all-to-all-start.2 = ((bf16[16,2,49152]{2,1,0:T(2,128)(2,1)}), bf16[16,2,49152]{2,1,0:T(2,128)(2,1)S(1)}, u32[]{:S(2)}, u32[]{:S(2)}) async-start(bf16[16,2,49152]{2,1,0:T(2,128)(2,1)} %reshape.299), calls=%async_computation.2 | async-start | bytes 6291456 | tf_op jit(solution)/shard_map/all_to_all | solution.py:68
  722.1 1.7 copy-start.3
  723.8 85.1 %all-to-all-start.11 = ((bf16[16,2,24576]{2,1,0:T(2,128)(2,1)}), bf16[16,2,24576]{2,1,0:T(2,128)(2,1)}, u32[]{:S(2)}, u32[]{:S(2)}) async-start(bf16[16,2,24576]{2,1,0:T(2,128)(2,1)} %reshape.307), calls=%async_computation.12 | async-start | bytes 3145728 | tf_op jit(solution)/shard_map/all_to_all | solution.py:68
  756.9 3.0 copy-start.4
  788.8 8.1 copy-start.11
  796.8 6.5 copy-start.8
  802.2 0.9 copy-start.20
  802.2 1.2 copy-start.22
  808.9 94.5 %all-to-all-start.7 = ((bf16[16,72,2048]{2,1,0:T(8,128)(2,1)}), bf16[16,72,2048]{2,1,0:T(8,128)(2,1)}, u32[]{:S(2)}, u32[]{:S(2)}) async-start(bf16[16,72,2048]{2,1,0:T(8,128)(2,1)} %bitcast.88), calls=%async_computation.7 | async-start | bytes 9437184 | tf_op jit(solution)/shard_map/all_to_all | solution.py:132
  816.0 186.0 %reduce-scatter.5.cloned.1.call-start = ((), (), s32[]{:S(2)}) async-start(), calls=%async_computation.19 | async-start | bytes 2359296 | tf_op jit(solution)/shard_map/reduce_scatter | solution.py:143
  903.4 21.1 %copy-start.21 = (bf16[1152,384]{0,1:T(8,128)(2,1)S(1)}, bf16[1152,384]{0,1:T(8,128)(2,1)}, u32[]{:S(2)}) copy-start(bf16[1152,384]{0,1:T(8,128)(2,1)} %copy-done.20) | copy-start | bytes 2654212
  903.4 21.2 %copy-start.23 = (bf16[1152,384]{0,1:T(8,128)(2,1)S(1)}, bf16[1152,384]{0,1:T(8,128)(2,1)}, u32[]{:S(2)}) copy-start(bf16[1152,384]{0,1:T(8,128)(2,1)} %copy-done.22) | copy-start | bytes 2654212
  903.4 120.0 %all-to-all-start.5 = ((bf16[16,72,2048]{2,1,0:T(8,128)(2,1)}), bf16[16,72,2048]{2,1,0:T(8,128)(2,1)}, u32[]{:S(2)}, u32[]{:S(2)}) async-start(bf16[16,72,2048]{2,1,0:T(8,128)(2,1)} %bitcast.87), calls=%async_computation.5 | async-start | bytes 9437184 | tf_op jit(solution)/shard_map/all_to_all | solution.py:126
  924.5 81.6 %reduce-scatter.3.cloned.1.call-start = ((), (), s32[]{:S(2)}) async-start(), calls=%async_computation.18 | async-start | bytes 4718592 | tf_op jit(solution)/shard_map/reduce_scatter | solution.py:140
  1001.9 4.2 copy-start.5
  1035.2 5.3 copy-start.2
  1035.2 10.0 copy-start.1
Sparse Core Ops, SparseCore 0:
  822.4 10.2 reduce-scatter.4
  933.7 12.1 reduce-scatter.2
where the time goes:
time: 1070 us; the launch traced here: 1050 us
  waiting for transfers between devices  401 us (37%)
  local copies, waits for them, and re-layouts  236 us (22%)
  other arithmetic  187 us (17%)
  starting transfers between devices  169 us (16%)
  matrix products  45 us (4%)
  between operations  14.8 us (1%)
    unnamed x78, local copies, waits for them, and re-layouts  150 us
    all_to_all x6, waiting for transfers between devices, relocate(): lax.all_to_all(as_sent(flats), 'expert', split_axis=0, concat_axis=0, til...  106 us
    all_to_all x6, waiting for transfers between devices, relocate(): lax.all_to_all(as_sent(ordered), 'expert', split_axis=0, concat_axis=0, t...  80.5 us
    all_to_all x1, waiting for transfers between devices, per_device(): lax.all_to_all(row_grad.reshape(count, capacity, width), 'expert', split_...  76.9 us
    all_to_all x1, waiting for transfers between devices, per_device(): lax.all_to_all(send_cot, 'expert', split_axis=0, concat_axis=0, tiled=True)  76.1 us
    all_to_all x6, starting transfers between devices, relocate(): lax.all_to_all(as_sent(ordered), 'expert', split_axis=0, concat_axis=0, t...  69 us
    all_to_all x6, other arithmetic, relocate(): lax.all_to_all(as_sent(flats), 'expert', split_axis=0, concat_axis=0, til...  66.9 us
    all_to_all x1, waiting for transfers between devices, per_device(): lax.all_to_all(send_x, 'expert', split_axis=0, concat_axis=0, tiled=True)  61.2 us
  transfers between devices with their start and end apart: 18, of which 11 were waited for; matrix products, arithmetic and copies ran while one was open for 38% of the time, Pallas kernels for 0%

commit v1 on v0

--- a/solution.py
+++ b/solution.py
@@ -6,10 +6,6 @@
 beta_one = 0.9
 beta_two = 0.95
 epsilon = 1e-08
-
-
-def as_sent(array):
-    return jax.tree.map(lambda a: a.astype(jnp.bfloat16) if a.dtype == jnp.float32 else a, array)
 
 
 def expert_forward(rows_x, w_gu, w_down):
@@ -55,54 +51,26 @@
     )
 
 
-def relocate(blocks, source, count):
-    flats = tuple((block.reshape(count, -1) for block in blocks))
-    spread = jax.tree.map(
-        lambda part, own: part.astype(own.dtype),
-        lax.all_to_all(as_sent(flats), "expert", split_axis=0, concat_axis=0, tiled=True),
-        flats,
+def spread(block, count):
+    part = block.shape[0] // count
+    return lax.all_to_all(
+        block.reshape(count, part, block.shape[1]), "expert", split_axis=0, concat_axis=0, tiled=True
     )
-    ordered = tuple((jnp.take(piece, source, axis=0) for piece in spread))
-    landed = jax.tree.map(
-        lambda part, own: part.astype(own.dtype),
-        lax.all_to_all(as_sent(ordered), "expert", split_axis=0, concat_axis=0, tiled=True),
-        ordered,
-    )
-    return tuple((piece.reshape(block.shape) for piece, block in zip(landed, blocks)))
 
 
-def per_device(
-    tokens,
-    out_grad,
-    expert_ids,
-    route_scores,
-    old_slot,
-    new_slot,
-    gate_up,
-    down,
-    first_gu,
-    second_gu,
-    first_down,
-    second_down,
-):
+def land(pieces, source):
+    ordered = jnp.take(pieces, source, axis=0)
+    back = lax.all_to_all(ordered, "expert", split_axis=0, concat_axis=0, tiled=True)
+    return back.reshape(-1, back.shape[2])
+
+
+def rows_by_exchange(tokens, out_grad, target, probs, w_gu, w_down):
     count = lax.axis_size("expert")
     tok_rows, width = tokens.shape
-    top = expert_ids.shape[1]
+    top = target.shape[1]
     capacity = max(2, tok_rows * top * 9 // (8 * count))
     rows = count * capacity
     lanes = jnp.arange(count, dtype=jnp.int32)
-    owner = new_slot[None, :] == lanes[:, None]
-    source = jnp.sum(jnp.where(owner, old_slot[None, :], 0), axis=1)
-    moments = (first_gu, second_gu, first_down, second_down)
-    moved = relocate((gate_up, down) + moments, source, count)
-    state = moved[2:]
-    w_gu = moved[0][0]
-    w_down = moved[1][0]
-    probs = route_scores / jnp.sum(route_scores, axis=1, keepdims=True)
-    target = jnp.sum(
-        jnp.where(expert_ids[:, :, None] == lanes[None, None, :], new_slot[None, None, :], 0),
-        axis=2,
-    )
     flat_target = target.reshape(-1)
     onehot = (flat_target[:, None] == lanes[None, :]).astype(jnp.int32)
     place = jnp.sum(onehot * (jnp.cumsum(onehot, axis=0) - 1), axis=1)
@@ -132,10 +100,45 @@
     back_grad = lax.all_to_all(
         row_grad.reshape(count, capacity, width), "expert", split_axis=0, concat_axis=0, tiled=True
     )
-    got_out = jnp.take(back_out.reshape(rows, width), slot, axis=0).reshape(tok_rows, top, width)
-    got_grad = jnp.take(back_grad.reshape(rows, width), slot, axis=0).reshape(tok_rows, top, width)
-    mixed = jnp.sum(probs[:, :, None] * got_out.astype(jnp.float32), axis=1).astype(jnp.bfloat16)
-    token_grad = jnp.sum(got_grad.astype(jnp.float32), axis=1).astype(jnp.bfloat16)
+    back_pick = lambda weight, piece: lax.dot_general(
+        weight.astype(jnp.bfloat16),
+        piece.reshape(rows, width),
+        (((0,), (0,)), ((), ())),
+        preferred_element_type=jnp.float32,
+    )
+    weight = pick.astype(jnp.float32) * slot_prob[:, None]
+    coarse = lax.reduce_precision(weight, 8, 7)
+    mixed = (back_pick(coarse, back_out) + back_pick(weight - coarse, back_out)).astype(jnp.bfloat16)
+    token_grad = back_pick(pick, back_grad).astype(jnp.bfloat16)
+    return (mixed, token_grad, grad_gu, grad_down)
+
+
+def per_device(
+    tokens,
+    out_grad,
+    expert_ids,
+    route_scores,
+    old_slot,
+    new_slot,
+    gate_up,
+    down,
+    first_gu,
+    second_gu,
+    first_down,
+    second_down,
+):
+    count = lax.axis_size("expert")
+    lanes = jnp.arange(count, dtype=jnp.int32)
+    owner = new_slot[None, :] == lanes[:, None]
+    source = jnp.sum(jnp.where(owner, old_slot[None, :], 0), axis=1)
+    probs = route_scores / jnp.sum(route_scores, axis=1, keepdims=True)
+    target = jnp.sum(
+        jnp.where(expert_ids[:, :, None] == lanes[None, None, :], old_slot[None, None, :], 0),
+        axis=2,
+    )
+    mixed, token_grad, grad_gu, grad_down = rows_by_exchange(
+        tokens, out_grad, target, probs, gate_up[0], down[0]
+    )
     share_gu, share_down = (
         lax.psum_scatter(
             grad_gu.astype(jnp.bfloat16), "dp", scatter_dimension=0, tiled=True
@@ -144,8 +147,10 @@
             grad_down.astype(jnp.bfloat16), "dp", scatter_dimension=1, tiled=True
         ).astype(jnp.float32),
     )
-    update_gu = adam_direction(state[0][0], state[1][0], share_gu)[None]
-    update_down = adam_direction(state[2][0], state[3][0], share_down)[None]
+    step_gu = adam_direction(first_gu[0], second_gu[0], share_gu)
+    step_down = adam_direction(first_down[0], second_down[0], share_down)
+    update_gu = land(spread(step_gu, count), source)[None]
+    update_down = land(spread(step_down, count), source)[None]
     return (mixed, token_grad, update_gu, update_down)
 
 

time: 1070 us -> 641 us (0.60); the launches traced: 1050 us -> 638 us
  local copies, waits for them, and re-layouts: 236 us -> 9.84 us
  other arithmetic: 187 us -> 22.7 us
  starting transfers between devices: 169 us -> 98.4 us
  waiting for transfers between devices: 401 us -> 429 us
  matrix products: 45 us -> 64.1 us
    unnamed x78 -> x24, local copies, waits for them, and re-layouts: 150 us -> 5.69 us
    all_to_all x15 -> x0, other arithmetic: 118 us -> none  [the longest x6 66.9 us: relocate(): lax.all_to_all(as_sent(flats), 'expert', split_axis=0, concat_axis=0, til...]
    all_to_all x16 -> x8, starting transfers between devices: 169 us -> 98.1 us  [the longest x2 28.1 us: spread(): lax.all_to_all(block.reshape(count, part, block.shape[1]), 'expert', spli...]
    gather x8 -> x2, local copies, waits for them, and re-layouts: 39.1 us -> 3.26 us  [land(): ordered = jnp.take(pieces, source, axis=0)]
    mul x4 -> x0, other arithmetic: 33 us -> none  [the longest x2 16.5 us: adam_direction(): first_new = beta_one * first.astype(jnp.float32) + (1.0 - beta_one) * grad]
    all_to_all x7 -> x0, local copies, waits for them, and re-layouts: 31 us -> none  [relocate(): lax.all_to_all(as_sent(flats), 'expert', split_axis=0, concat_axis=0, til...]
    reduce_scatter x1, waiting for transfers between devices: 0.02 us -> 25.3 us  [per_device(): lax.psum_scatter(grad_down.astype(jnp.bfloat16), 'dp', scatter_dimension=...]
    dot_general x2 -> x5, matrix products: 7.07 us -> 20.8 us  [the longest x3 11.6 us: rows_by_exchange(): lax.dot_general(weight.astype(jnp.bfloat16), piece.reshape(rows, width),...]
  transfers between devices with their start and end apart: 18 -> 10, of which waited for: 11 -> 10; matrix products, arithmetic and copies ran while one was open for 38% -> 8% of each run, Pallas kernels for 0% -> 0%
where the time goes in v1:
time: 641 us; the launch traced here: 638 us
  waiting for transfers between devices  429 us (67%)
  starting transfers between devices  98.4 us (15%)
  matrix products  64.1 us (10%)
  other arithmetic  22.7 us (4%)
  between operations  14.3 us (2%)
  local copies, waits for them, and re-layouts  9.84 us (2%)
    all_to_all x1, waiting for transfers between devices, rows_by_exchange(): lax.all_to_all(output.reshape(count, capacity, width), 'expert', split_ax...  85.6 us
    all_to_all x1, waiting for transfers between devices, rows_by_exchange(): lax.all_to_all(send_x, 'expert', split_axis=0, concat_axis=0, tiled=True)  83.8 us
    all_to_all x1, waiting for transfers between devices, rows_by_exchange(): lax.all_to_all(send_cot, 'expert', split_axis=0, concat_axis=0, tiled=True)  79 us
    all_to_all x1, waiting for transfers between devices, rows_by_exchange(): lax.all_to_all(row_grad.reshape(count, capacity, width), 'expert', split_...  61 us
    all_to_all x2, waiting for transfers between devices, spread(): lax.all_to_all(block.reshape(count, part, block.shape[1]), 'expert', spli...  48 us
    all_to_all x2, waiting for transfers between devices, land(): lax.all_to_all(ordered, 'expert', split_axis=0, concat_axis=0, tiled=True)  33.5 us
    all_to_all x2, starting transfers between devices, spread(): lax.all_to_all(block.reshape(count, part, block.shape[1]), 'expert', spli...  28.1 us
    all_to_all x2, starting transfers between devices, land(): lax.all_to_all(ordered, 'expert', split_axis=0, concat_axis=0, tiled=True)  26.7 us
  transfers between devices with their start and end apart: 10, of which 10 were waited for; matrix products, arithmetic and copies ran while one was open for 8% of the time, Pallas kernels for 0%

profile of v1, /device:TPU:0, one launch (start us, length us, event | category | flops | bytes accessed | tf_op | source)
XLA Modules:
  0.0 637.9 jit_solution(15172040724270208581)
XLA Ops:
  7.2 0.0 copy-start
  7.2 0.9 select_reduce_fusion.1
  8.1 0.1 copy.23
  8.2 0.1 eq.74
  8.3 0.1 eq.78
  8.4 4.5 reduce-window.6
  12.9 0.1 slice.22
  13.0 0.1 copy.25
  13.2 0.1 copy.26
  13.3 0.1 add_add_fusion
  13.4 0.1 reduce_sum.51
  13.5 4.2 fusion.1
  17.7 4.6 convolution_convert_fusion.2
  22.3 8.5 %all-to-all-start = ((bf16[16,72,2048]{2,1,0:T(8,128)(2,1)}), bf16[16,72,2048]{2,1,0:T(8,128)(2,1)}, u32[]{:S(2)}, u32[]{:S(2)}) async-start(bf16[16,72,2048]{2,1,0:T(8,128)(2,1)} %bitcast.72), calls=%async_computation | async-start | bytes 9437184 | tf_op jit(solution)/shard_map/all_to_all | solution.py:91
  30.8 0.0 copy-done.4
  30.9 0.1 copy.28
  31.0 0.1 broadcast_in_dim.72
  31.1 0.6 select_reduce_fusion
  31.6 4.7 fusion
  36.3 83.8 %all-to-all-done = bf16[16,72,2048]{2,1,0:T(8,128)(2,1)} async-done(((bf16[16,72,2048]{2,1,0:T(8,128)(2,1)}), bf16[16,72,2048]{2,1,0:T(8,128)(2,1)}, u32[]{:S(2)}, u32[]{:S(2)}) %all-to-all-start) | async-done | bytes 4718624 | tf_op jit(solution)/shard_map/all_to_all | solution.py:91
  120.1 22.4 %all-to-all-start.2 = ((bf16[16,72,2048]{2,1,0:T(8,128)(2,1)}), bf16[16,72,2048]{2,1,0:T(8,128)(2,1)}, u32[]{:S(2)}, u32[]{:S(2)}) async-start(bf16[16,72,2048]{2,1,0:T(8,128)(2,1)} %bitcast.73), calls=%async_computation.2 | async-start | bytes 9437184 | tf_op jit(solution)/shard_map/all_to_all | solution.py:97
  142.5 0.2 reduce-scatter.5.cloned.1.call-start
  142.7 0.0 copy-done
  142.7 8.4 %fusion.10 = f32[1152,768]{0,1:T(8,128)} fusion(bf16[1152,2048]{1,0:T(8,128)(2,1)} %bitcast.3, bf16[1,2048,768]{2,1,0:T(8,128)(2,1)S(1)} %copy-done), kind=kOutput, calls=%fused_computation.22 | convolution fusion | flops 3623878656 | bytes 11403264 | tf_op jit(solution)/shard_map/dot_general | solution.py:13
  151.1 79.0 %all-to-all-done.2 = bf16[16,72,2048]{2,1,0:T(8,128)(2,1)} async-done(((bf16[16,72,2048]{2,1,0:T(8,128)(2,1)}), bf16[16,72,2048]{2,1,0:T(8,128)(2,1)}, u32[]{:S(2)}, u32[]{:S(2)}) %all-to-all-start.2) | async-done | bytes 4718624 | tf_op jit(solution)/shard_map/all_to_all | solution.py:97
  230.1 7.7 %multiply_convert_fusion.1 = (bf16[1152,384]{0,1:T(8,128)(2,1)}, bf16[1152,384]{0,1:T(8,128)(2,1)}, bf16[1152,384]{0,1:T(8,128)(2,1)S(1)}) fusion(f32[1152,768]{0,1:T(8,128)} %fusion.10, bf16[1152,2048]{1,0:T(8,128)(2,1)} %bitcast.9, bf16[1,384,2048]{2,1,0:T(8,128)(2,1)} %param.19), kind=kOutput, calls=%fused_computation.33 | convolution fusion | flops 1819017216 | bytes 12484608 | tf_op jit(solution)/shard_map/dot_general | solution.py:26
  237.8 0.9 copy-done.8
  238.8 5.7 convolution_convert_fusion.4
  244.4 0.0 reduce-scatter.5.cloned.1.call-update
  244.5 25.3 %reduce-scatter.5.cloned.1.call-done = bf16[384,1024]{1,0:T(8,128)(2,1)} async-done(((bf16[384,2048]{1,0:T(8,128)(2,1)}), bf16[384,1024]{1,0:T(8,128)(2,1)}) %reduce-scatter.5.cloned.1.call-update) | async-done | bytes 786448 | tf_op jit(solution)/shard_map/reduce_scatter | solution.py:146
  269.8 3.7 fusion.24
  273.5 6.9 %all-to-all-start.6 = ((bf16[16,24,1024]{2,1,0:T(8,128)(2,1)}), bf16[16,24,1024]{2,1,0:T(8,128)(2,1)}, u32[]{:S(2)}, u32[]{:S(2)}) async-start(bf16[16,24,1024]{2,1,0:T(8,128)(2,1)} %bitcast.76), calls=%async_computation.8 | async-start | bytes 1572864 | tf_op jit(solution)/shard_map/all_to_all | solution.py:56
  280.4 0.0 copy-done.5
  280.4 0.0 copy-done.7
  280.4 0.1 select_reduce_fusion.2
  280.5 20.0 %all-to-all-done.6 = bf16[16,24,1024]{2,1,0:T(8,128)(2,1)} async-done(((bf16[16,24,1024]{2,1,0:T(8,128)(2,1)}), bf16[16,24,1024]{2,1,0:T(8,128)(2,1)}, u32[]{:S(2)}, u32[]{:S(2)}) %all-to-all-start.6) | async-done | bytes 786464 | tf_op jit(solution)/shard_map/all_to_all | solution.py:56
  300.5 2.6 gather_fusion.1
  303.1 2.1 broadcast_select_fusion.1
  305.2 5.1 all-to-all-start.7
  310.3 7.1 %convolution_convert_fusion = bf16[1152,2048]{1,0:T(8,128)(2,1)} fusion(bf16[1,2048,768]{2,1,0:T(8,128)(2,1)S(1)} %copy-done, bf16[1152,384]{0,1:T(8,128)(2,1)} %get-tuple-element.5, bf16[1152,384]{0,1:T(8,128)(2,1)} %get-tuple-element.4), kind=kOutput, calls=%fused_computation.4 | convolution fusion | flops 3629776896 | bytes 9633792 | tf_op jit(solution)/shard_map/dot_general | solution.py:32
  317.4 11.7 %all-to-all-done.7 = bf16[16,24,1024]{2,1,0:T(8,128)(2,1)} async-done(((bf16[16,24,1024]{2,1,0:T(8,128)(2,1)}), bf16[16,24,1024]{2,1,0:T(8,128)(2,1)}, u32[]{:S(2)}, u32[]{:S(2)}) %all-to-all-start.7) | async-done | bytes 786464 | tf_op jit(solution)/shard_map/all_to_all | solution.py:63
  329.1 5.1 all-to-all-start.3
  334.2 0.0 reduce-scatter.3.cloned.1.call-start
  334.3 8.9 %convolution_convert_fusion.3 = bf16[2048,768]{1,0:T(8,128)(2,1)} fusion(bf16[1152,2048]{1,0:T(8,128)(2,1)} %bitcast.3, bf16[1152,384]{0,1:T(8,128)(2,1)S(1)} %copy-done.10, bf16[1152,384]{0,1:T(8,128)(2,1)S(1)} %copy-done.9), kind=kOutput, calls=%fused_computation.13 | convolution fusion | flops 3628990464 | bytes 9633792 | tf_op jit(solution)/shard_map/dot_general | solution.py:35
  343.2 0.0 reduce-scatter.3.cloned.1.call-update
  343.2 12.3 %reduce-scatter.3.cloned.1.call-done = bf16[1024,768]{1,0:T(8,128)(2,1)} async-done(((bf16[2048,768]{1,0:T(8,128)(2,1)}), bf16[1024,768]{1,0:T(8,128)(2,1)}) %reduce-scatter.3.cloned.1.call-update) | async-done | bytes 1572880 | tf_op jit(solution)/shard_map/reduce_scatter | solution.py:143
  355.5 0.0 copy-done.3
  355.5 5.0 fusion.12
  360.5 61.0 %all-to-all-done.3 = bf16[16,72,2048]{2,1,0:T(8,128)(2,1)} async-done(((bf16[16,72,2048]{2,1,0:T(8,128)(2,1)}), bf16[16,72,2048]{2,1,0:T(8,128)(2,1)}, u32[]{:S(2)}, u32[]{:S(2)}) %all-to-all-start.3) | async-done | bytes 4718624 | tf_op jit(solution)/shard_map/all_to_all | solution.py:100
  421.6 21.3 %all-to-all-start.4 = ((bf16[16,64,768]{2,1,0:T(8,128)(2,1)}), bf16[16,64,768]{2,1,0:T(8,128)(2,1)S(1)}, u32[]{:S(2)}, u32[]{:S(2)}) async-start(bf16[16,64,768]{2,1,0:T(8,128)(2,1)} %bitcast.14), calls=%async_computation.5 | async-start | bytes 3145728 | tf_op jit(solution)/shard_map/all_to_all | solution.py:56
  442.8 5.5 convolution_convert_fusion.1
  448.4 28.1 %all-to-all-done.4 = bf16[16,64,768]{2,1,0:T(8,128)(2,1)S(1)} async-done(((bf16[16,64,768]{2,1,0:T(8,128)(2,1)}), bf16[16,64,768]{2,1,0:T(8,128)(2,1)S(1)}, u32[]{:S(2)}, u32[]{:S(2)}) %all-to-all-start.4) | async-done | bytes 1572896 | tf_op jit(solution)/shard_map/all_to_all | solution.py:56
  476.4 7.3 %all-to-all-start.1 = ((bf16[16,72,2048]{2,1,0:T(8,128)(2,1)}), bf16[16,72,2048]{2,1,0:T(8,128)(2,1)}, u32[]{:S(2)}, u32[]{:S(2)}) async-start(bf16[16,72,2048]{2,1,0:T(8,128)(2,1)} %bitcast.75), calls=%async_computation.1 | async-start | bytes 9437184 | tf_op jit(solution)/shard_map/all_to_all | solution.py:94
  483.8 0.6 gather_fusion
  484.5 1.4 broadcast_select_fusion
  485.8 85.6 %all-to-all-done.1 = bf16[16,72,2048]{2,1,0:T(8,128)(2,1)} async-done(((bf16[16,72,2048]{2,1,0:T(8,128)(2,1)}), bf16[16,72,2048]{2,1,0:T(8,128)(2,1)}, u32[]{:S(2)}, u32[]{:S(2)}) %all-to-all-start.1) | async-done | bytes 4718624 | tf_op jit(solution)/shard_map/all_to_all | solution.py:94
  571.4 21.6 %all-to-all-start.5 = ((bf16[16,64,768]{2,1,0:T(8,128)(2,1)}), bf16[16,64,768]{2,1,0:T(8,128)(2,1)}, u32[]{:S(2)}, u32[]{:S(2)}) async-start(bf16[16,64,768]{2,1,0:T(8,128)(2,1)} %broadcast_select_fusion), calls=%async_computation.6 | async-start | bytes 3145728 | tf_op jit(solution)/shard_map/all_to_all | solution.py:63
  593.0 4.0 convolution_convert_fusion.5
  597.1 3.3 fusion.27
  600.4 0.0 copy-start.1
  600.4 4.3 fusion.13
  604.6 21.7 %all-to-all-done.5 = bf16[16,64,768]{2,1,0:T(8,128)(2,1)} async-done(((bf16[16,64,768]{2,1,0:T(8,128)(2,1)}), bf16[16,64,768]{2,1,0:T(8,128)(2,1)}, u32[]{:S(2)}, u32[]{:S(2)}) %all-to-all-start.5) | async-done | bytes 1572896 | tf_op jit(solution)/shard_map/all_to_all | solution.py:63
  626.4 2.7 copy.33
  629.0 2.1 copy.34
  (26 shorter events, 0.2 us)
Async XLA Ops:
  7.2 135.5 %copy-start = (bf16[1,2048,768]{2,1,0:T(8,128)(2,1)S(1)}, bf16[1,2048,768]{2,1,0:T(8,128)(2,1)}, u32[]{:S(2)}) copy-start(bf16[1,2048,768]{2,1,0:T(8,128)(2,1)} %param.18) | copy-start | bytes 9437188
  22.3 8.5 %copy-start.4 = (f32[128,8]{0,1:T(8,128)S(1)}, f32[128,8]{0,1:T(8,128)}, u32[]{:S(2)}) copy-start(f32[128,8]{0,1:T(8,128)} %param.15) | copy-start | bytes 12292
  22.3 97.8 %all-to-all-start = ((bf16[16,72,2048]{2,1,0:T(8,128)(2,1)}), bf16[16,72,2048]{2,1,0:T(8,128)(2,1)}, u32[]{:S(2)}, u32[]{:S(2)}) async-start(bf16[16,72,2048]{2,1,0:T(8,128)(2,1)} %bitcast.72), calls=%async_computation | async-start | bytes 9437184 | tf_op jit(solution)/shard_map/all_to_all | solution.py:91
  120.1 110.0 %all-to-all-start.2 = ((bf16[16,72,2048]{2,1,0:T(8,128)(2,1)}), bf16[16,72,2048]{2,1,0:T(8,128)(2,1)}, u32[]{:S(2)}, u32[]{:S(2)}) async-start(bf16[16,72,2048]{2,1,0:T(8,128)(2,1)} %bitcast.73), calls=%async_computation.2 | async-start | bytes 9437184 | tf_op jit(solution)/shard_map/all_to_all | solution.py:97
  142.5 127.3 %reduce-scatter.5.cloned.1.call-start = ((), (), s32[]{:S(2)}) async-start(), calls=%async_computation.11 | async-start | bytes 2359296 | tf_op jit(solution)/shard_map/reduce_scatter | solution.py:146
  237.8 0.9 copy-start.8
  244.4 35.9 %copy-start.5 = (s32[16]{0:T(128)S(1)}, s32[16]{0:T(128)}, u32[]{:S(2)}) copy-start(s32[16]{0:T(128)} %param.16) | copy-start | bytes 196
  244.4 35.9 %copy-start.7 = (s32[16]{0:T(128)S(1)}, s32[16]{0:T(128)}, u32[]{:S(2)}) copy-start(s32[16]{0:T(128)} %param.17) | copy-start | bytes 196
  273.5 27.0 %all-to-all-start.6 = ((bf16[16,24,1024]{2,1,0:T(8,128)(2,1)}), bf16[16,24,1024]{2,1,0:T(8,128)(2,1)}, u32[]{:S(2)}, u32[]{:S(2)}) async-start(bf16[16,24,1024]{2,1,0:T(8,128)(2,1)} %bitcast.76), calls=%async_computation.8 | async-start | bytes 1572864 | tf_op jit(solution)/shard_map/all_to_all | solution.py:56
  305.2 23.9 %all-to-all-start.7 = ((bf16[16,24,1024]{2,1,0:T(8,128)(2,1)}), bf16[16,24,1024]{2,1,0:T(8,128)(2,1)}, u32[]{:S(2)}, u32[]{:S(2)}) async-start(bf16[16,24,1024]{2,1,0:T(8,128)(2,1)} %broadcast_select_fusion.1), calls=%async_computation.9 | async-start | bytes 1572864 | tf_op jit(solution)/shard_map/all_to_all | solution.py:63
  329.1 5.1 copy-start.9
  329.1 5.1 copy-start.10
  329.1 92.4 %all-to-all-start.3 = ((bf16[16,72,2048]{2,1,0:T(8,128)(2,1)}), bf16[16,72,2048]{2,1,0:T(8,128)(2,1)}, u32[]{:S(2)}, u32[]{:S(2)}) async-start(bf16[16,72,2048]{2,1,0:T(8,128)(2,1)} %bitcast.74), calls=%async_computation.3 | async-start | bytes 9437184 | tf_op jit(solution)/shard_map/all_to_all | solution.py:100
  334.2 21.3 %reduce-scatter.3.cloned.1.call-start = ((), (), s32[]{:S(2)}) async-start(), calls=%async_computation.10 | async-start | bytes 4718592 | tf_op jit(solution)/shard_map/reduce_scatter | solution.py:143
  343.2 12.3 %copy-start.2 = (bf16[1,1024,768]{2,1,0:T(8,128)(2,1)S(1)}, bf16[1,1024,768]{2,1,0:T(8,128)(2,1)}, u32[]{:S(2)}) copy-start(bf16[1,1024,768]{2,1,0:T(8,128)(2,1)} %param.21) | copy-start | bytes 4718596
  343.2 12.3 %copy-start.3 = (bf16[1,1024,768]{2,1,0:T(8,128)(2,1)S(1)}, bf16[1,1024,768]{2,1,0:T(8,128)(2,1)}, u32[]{:S(2)}) copy-start(bf16[1,1024,768]{2,1,0:T(8,128)(2,1)} %param.20) | copy-start | bytes 4718596
  360.5 82.3 %copy-start.6 = (bf16[1,384,2048]{2,1,0:T(8,128)(2,1)S(1)}, bf16[1,384,2048]{2,1,0:T(8,128)(2,1)}, u32[]{:S(2)}) copy-start(bf16[1,384,2048]{2,1,0:T(8,128)(2,1)} %param.19) | copy-start | bytes 4718596
  421.6 54.9 %all-to-all-start.4 = ((bf16[16,64,768]{2,1,0:T(8,128)(2,1)}), bf16[16,64,768]{2,1,0:T(8,128)(2,1)S(1)}, u32[]{:S(2)}, u32[]{:S(2)}) async-start(bf16[16,64,768]{2,1,0:T(8,128)(2,1)} %bitcast.14), calls=%async_computation.5 | async-start | bytes 3145728 | tf_op jit(solution)/shard_map/all_to_all | solution.py:56
  476.4 94.9 %all-to-all-start.1 = ((bf16[16,72,2048]{2,1,0:T(8,128)(2,1)}), bf16[16,72,2048]{2,1,0:T(8,128)(2,1)}, u32[]{:S(2)}, u32[]{:S(2)}) async-start(bf16[16,72,2048]{2,1,0:T(8,128)(2,1)} %bitcast.75), calls=%async_computation.1 | async-start | bytes 9437184 | tf_op jit(solution)/shard_map/all_to_all | solution.py:94
  571.4 55.0 %all-to-all-start.5 = ((bf16[16,64,768]{2,1,0:T(8,128)(2,1)}), bf16[16,64,768]{2,1,0:T(8,128)(2,1)}, u32[]{:S(2)}, u32[]{:S(2)}) async-start(bf16[16,64,768]{2,1,0:T(8,128)(2,1)} %broadcast_select_fusion), calls=%async_computation.6 | async-start | bytes 3145728 | tf_op jit(solution)/shard_map/all_to_all | solution.py:63
  600.4 30.7 %copy-start.1 = (bf16[1,2048,768]{2,1,0:T(8,128)(2,1)S(1)}, bf16[1,2048,768]{2,1,0:T(8,128)(2,1)}, u32[]{:S(2)}) copy-start(bf16[1,2048,768]{2,1,0:T(8,128)(2,1)} %param.18) | copy-start | bytes 9437188
Sparse Core Ops, SparseCore 0:
  244.6 25.1 reduce-scatter.4
  343.3 12.1 reduce-scatter.2

commit v2 on v1

--- a/solution.py
+++ b/solution.py
@@ -1,7 +1,15 @@
+import functools
+
 import jax
 import jax.numpy as jnp
 from jax import lax
+from jax.experimental import pallas as pl
+from jax.experimental.pallas import tpu as pltpu
 from jax.sharding import PartitionSpec as P
+
+MESH = pl.DeviceIdType.MESH
+SIDE = 2
+PLANE = SIDE * SIDE
 
 beta_one = 0.9
 beta_two = 0.95
@@ -62,6 +70,260 @@
     ordered = jnp.take(pieces, source, axis=0)
     back = lax.all_to_all(ordered, "expert", split_axis=0, concat_axis=0, tiled=True)
     return back.reshape(-1, back.shape[2])
+
+
+def position(count):
+    deep = count // PLANE
+    me = lax.axis_index("expert")
+    return (deep, me // PLANE, (me // SIDE) % SIDE, me % SIDE)
+
+
+def slot_of(z, y, x):
+    return z * PLANE + y * SIDE + x
+
+
+def greet(partners):
+    barrier = pltpu.get_barrier_semaphore()
+    for partner in partners:
+        pl.semaphore_signal(barrier, inc=1, device_id=partner, device_id_type=MESH)
+    pl.semaphore_wait(barrier, len(partners))
+
+
+def gather_kernel(count, *refs):
+    tensors = 2
+    sources, outs = refs[:tensors], refs[tensors : 2 * tensors]
+    own_sem, z_send, z_recv, xy_send, xy_recv, d_send, d_recv = refs[2 * tensors :]
+    deep, z, y, x = position(count)
+    core = lax.axis_index("dp")
+    half = sources[0].shape[0] // 2
+    up = [(slot_of((z + k) % deep, y, x), core) for k in range(deep)]
+    beside = ((slot_of(z, y, 1 - x), core), (slot_of(z, 1 - y, x), core))
+    greet(up[1:] + list(beside))
+
+    def copy(src, dst, send, recv, device):
+        return pltpu.make_async_remote_copy(
+            src_ref=src, dst_ref=dst, send_sem=send, recv_sem=recv,
+            device_id=device, device_id_type=MESH,
+        )
+
+    def across(t, k, origin):
+        return copy(sources[t], outs[t].at[origin], z_send.at[t, k - 1], z_recv.at[t, k - 1], up[k])
+
+    def to_side(t, k, way, src, origin):
+        return copy(
+            src, outs[t].at[origin], xy_send.at[t, k, way], xy_recv.at[t, k, way], beside[way]
+        )
+
+    def onward(t, k, way, origin):
+        rows = pl.ds(way * half, half)
+        piece = outs[t].at[origin, rows]
+        return copy(piece, piece, d_send.at[t, k, way], d_recv.at[t, k, way], beside[1 - way])
+
+    me = slot_of(z, y, x)
+    sent = []
+    locals_ = []
+    for t in range(tensors):
+        own = pltpu.make_async_copy(sources[t], outs[t].at[me], own_sem.at[t])
+        own.start()
+        locals_.append(own)
+    for t in range(tensors):
+        for way in range(2):
+            step = to_side(t, 0, way, sources[t], me)
+            step.start()
+            sent.append(step)
+        for k in range(1, deep):
+            step = across(t, k, me)
+            step.start()
+            sent.append(step)
+
+    def forward(t, k):
+        zk = (z - k + deep) % deep
+        came = (slot_of(zk, y, 1 - x), slot_of(zk, 1 - y, x))
+        for way in range(2):
+            to_side(t, k, way, outs[t].at[came[way]], came[way]).wait_recv()
+            step = onward(t, k, way, came[way])
+            step.start()
+            sent.append(step)
+
+    for t in range(tensors):
+        for k in range(1, deep):
+            origin = slot_of((z - k + deep) % deep, y, x)
+            across(t, k, origin).wait_recv()
+            for way in range(2):
+                step = to_side(t, k, way, outs[t].at[origin], origin)
+                step.start()
+                sent.append(step)
+            forward(t, k - 1)
+        forward(t, deep - 1)
+    for t in range(tensors):
+        for k in range(deep):
+            zk = (z - k + deep) % deep
+            for way in range(2):
+                onward(t, k, way, slot_of(zk, 1 - y, 1 - x)).wait_recv()
+    for own in locals_:
+        own.wait()
+    for step in sent:
+        step.wait_send()
+
+
+def gather_rows(tokens, out_grad):
+    count = lax.axis_size("expert")
+    rows, width = tokens.shape
+    deep = count // PLANE
+    dma = pltpu.SemaphoreType.DMA
+    full = jax.ShapeDtypeStruct((count, rows, width), tokens.dtype)
+    got = pl.pallas_call(
+        functools.partial(gather_kernel, count),
+        out_shape=(full, full),
+        in_specs=[pl.BlockSpec(memory_space=pl.ANY)] * 2,
+        out_specs=(pl.BlockSpec(memory_space=pl.ANY),) * 2,
+        scratch_shapes=[
+            dma((2,)),
+            dma((2, deep - 1)),
+            dma((2, deep - 1)),
+            dma((2, deep, 2)),
+            dma((2, deep, 2)),
+            dma((2, deep, 2)),
+            dma((2, deep, 2)),
+        ],
+        compiler_params=pltpu.CompilerParams(collective_id=0, has_side_effects=True),
+    )(tokens, out_grad)
+    return tuple(part.reshape(count * rows, width) for part in got)
+
+
+def sum_kernel(count, *refs):
+    tensors = 2
+    parts, outs = refs[:tensors], refs[tensors : 2 * tensors]
+    (got_d, got_xy, got_z, out_xy, out_z,
+     z_send, z_recv, xy_send, xy_recv, d_send, d_recv) = refs[2 * tensors :]
+    deep, z, y, x = position(count)
+    core = lax.axis_index("dp")
+    half = outs[0].shape[0] // 2
+    up = [(slot_of((z + k) % deep, y, x), core) for k in range(deep)]
+    beside = ((slot_of(z, y, 1 - x), core), (slot_of(z, 1 - y, x), core))
+    greet(up[1:] + list(beside))
+
+    def copy(src, dst, send, recv, device):
+        return pltpu.make_async_remote_copy(
+            src_ref=src, dst_ref=dst, send_sem=send, recv_sem=recv,
+            device_id=device, device_id_type=MESH,
+        )
+
+    def wide(ref, index):
+        return ref[index].astype(jnp.float32)
+
+    order = [(k + 1) % deep for k in range(deep)]
+    jobs = [(t, k) for t in range(tensors) for k in order]
+    sent = []
+    first = {}
+    for t, k in jobs:
+        far = slot_of((z + k) % deep, 1 - y, 1 - x)
+        for way in range(2):
+            step = copy(
+                parts[t].at[far, pl.ds(way * half, half)], got_d.at[t, k, way],
+                d_send.at[t, k, way], d_recv.at[t, k, way], beside[1 - way],
+            )
+            step.start()
+            first[t, k, way] = step
+            sent.append(step)
+    second = {}
+
+    def pass_on(t, k):
+        zk = (z + k) % deep
+        near = (slot_of(zk, y, 1 - x), slot_of(zk, 1 - y, x))
+        for way in range(2):
+            first[t, k, way].wait_recv()
+            rows, rest = pl.ds(way * half, half), pl.ds((1 - way) * half, half)
+            total = wide(parts[t], (near[way], rows)) + wide(got_d, (t, k, way))
+            out_xy[t, k, way, rows] = total.astype(jnp.bfloat16)
+            out_xy[t, k, way, rest] = parts[t][near[way], rest]
+            step = copy(
+                out_xy.at[t, k, way], got_xy.at[t, k, way],
+                xy_send.at[t, k, way], xy_recv.at[t, k, way], beside[way],
+            )
+            step.start()
+            second[t, k, way] = step
+            sent.append(step)
+
+    third = {}
+
+    def plane_sum(t, k):
+        second[t, k, 0].wait_recv()
+        second[t, k, 1].wait_recv()
+        total = wide(got_xy, (t, k, 0)) + wide(got_xy, (t, k, 1))
+        return total + wide(parts[t], slot_of((z + k) % deep, y, x))
+
+    def leave(t, k):
+        if k == 0:
+            return
+        out_z[t, k - 1] = plane_sum(t, k).astype(jnp.bfloat16)
+        step = copy(
+            out_z.at[t, k - 1], got_z.at[t, k - 1], z_send.at[t, k - 1], z_recv.at[t, k - 1], up[k]
+        )
+        step.start()
+        third[t, k] = step
+        sent.append(step)
+
+    pass_on(*jobs[0])
+    for now, after in zip(jobs, jobs[1:]):
+        pass_on(*after)
+        leave(*now)
+    for t in range(tensors):
+        total = plane_sum(t, 0)
+        for k in range(1, deep):
+            third[t, k].wait_recv()
+            total = total + wide(got_z, (t, k - 1))
+        outs[t][...] = total.astype(jnp.bfloat16)
+    for step in sent:
+        step.wait_send()
+
+
+def sum_rows(part_out, part_grad):
+    count = lax.axis_size("expert")
+    rows, width = part_out.shape[0] // count, part_out.shape[1]
+    deep = count // PLANE
+    dma = pltpu.SemaphoreType.DMA
+    block = jax.ShapeDtypeStruct((rows, width), part_out.dtype)
+    vmem = lambda *lead: pltpu.VMEM(lead + (width,), jnp.bfloat16)
+    return pl.pallas_call(
+        functools.partial(sum_kernel, count),
+        out_shape=(block, block),
+        in_specs=[pl.BlockSpec(memory_space=pltpu.VMEM)] * 2,
+        out_specs=(pl.BlockSpec(memory_space=pltpu.VMEM),) * 2,
+        scratch_shapes=[
+            vmem(2, deep, 2, rows // 2),
+            vmem(2, deep, 2, rows),
+            vmem(2, deep - 1, rows),
+            vmem(2, deep, 2, rows),
+            vmem(2, deep - 1, rows),
+            dma((2, deep - 1)),
+            dma((2, deep - 1)),
+            dma((2, deep, 2)),
+            dma((2, deep, 2)),
+            dma((2, deep, 2)),
+            dma((2, deep, 2)),
+        ],
+        compiler_params=pltpu.CompilerParams(
+            collective_id=1, has_side_effects=True, vmem_limit_bytes=56 * 1024 * 1024
+        ),
+    )(part_out.reshape(count, rows, width), part_grad.reshape(count, rows, width))
+
+
+def rows_by_gather(tokens, out_grad, target, probs, w_gu, w_down):
+    count = lax.axis_size("expert")
+    lanes = jnp.arange(count, dtype=jnp.int32)
+    chosen = target[:, :, None] == lanes[None, None, :]
+    weights = jnp.sum(jnp.where(chosen, probs[:, :, None], 0.0), axis=1).T
+    prob_in = lax.all_to_all(weights, "expert", split_axis=0, concat_axis=0, tiled=True)
+    rows_x, rows_g = gather_rows(tokens, out_grad)
+    prob = prob_in.reshape(-1, 1)
+    both, activated, output = expert_forward(rows_x, w_gu, w_down)
+    rows_cot = (prob * rows_g.astype(jnp.float32)).astype(jnp.bfloat16)
+    row_grad, grad_gu, grad_down = expert_backward(rows_x, rows_cot, both, activated, w_gu, w_down)
+    mixed, token_grad = sum_rows(
+        (prob * output.astype(jnp.float32)).astype(jnp.bfloat16), row_grad
+    )
+    return (mixed, token_grad, grad_gu, grad_down)
 
 
 def rows_by_exchange(tokens, out_grad, target, probs, w_gu, w_down):
@@ -136,7 +398,9 @@
         jnp.where(expert_ids[:, :, None] == lanes[None, None, :], old_slot[None, None, :], 0),
         axis=2,
     )
-    mixed, token_grad, grad_gu, grad_down = rows_by_exchange(
+    gathered = count % (2 * PLANE) == 0 and 2 * expert_ids.shape[1] >= count
+    rows_plan = rows_by_gather if gathered else rows_by_exchange
+    mixed, token_grad, grad_gu, grad_down = rows_plan(
         tokens, out_grad, target, probs, gate_up[0], down[0]
     )
     share_gu, share_down = (

time: 641 us -> 523 us (0.82)
  waiting for transfers between devices: 429 us -> 61.5 us
  Pallas kernels: 0 us -> 305 us
  starting transfers between devices: 98.4 us -> 34.2 us
  other arithmetic: 22.7 us -> 33.9 us
    all_to_all x4 -> x1, waiting for transfers between devices: 309 us -> 0.01 us  [rows_by_gather(): lax.all_to_all(weights, 'expert', split_axis=0, concat_axis=0, tiled=True)]
    pallas_call x0 -> x2, Pallas kernels: none -> 305 us  [the longest x1 162 us: sum_rows(): pl.pallas_call(functools.partial(sum_kernel, count), out_shape=(block, bl...]
    all_to_all x4 -> x1, starting transfers between devices: 43.3 us -> 8.31 us  [rows_by_gather(): lax.all_to_all(weights, 'expert', split_axis=0, concat_axis=0, tiled=True)]
    dot_general x5 -> x0, matrix products: 20.8 us -> none  [the longest x3 11.6 us: rows_by_exchange(): lax.dot_general(weight.astype(jnp.bfloat16), piece.reshape(rows, width),...]
    all_to_all x2, waiting for transfers between devices: 33.5 us -> 13 us  [land(): lax.all_to_all(ordered, 'expert', split_axis=0, concat_axis=0, tiled=True)]
    reduce_scatter x1, waiting for transfers between devices: 25.3 us -> 5.99 us  [per_device(): lax.psum_scatter(grad_down.astype(jnp.bfloat16), 'dp', scatter_dimension=...]
    convert_element_type x1 -> x2, other arithmetic: 0.01 us -> 16.2 us  [rows_by_gather(): rows_cot = (prob * rows_g.astype(jnp.float32)).astype(jnp.bfloat16)]
    all_to_all x2, starting transfers between devices: 28.1 us -> 13.4 us  [spread(): lax.all_to_all(block.reshape(count, part, block.shape[1]), 'expert', spli...]
  transfers between devices with their start and end apart: 10 -> 7, of which waited for: 10 -> 5; matrix products, arithmetic and copies ran while one was open for 8% -> 12% of each run, Pallas kernels for 0% -> 58%
where the time goes in v2:
time: 523 us; the launch traced here: 522 us
  Pallas kernels  305 us (58%)
  waiting for transfers between devices  61.5 us (12%)
  matrix products  57.8 us (11%)
  starting transfers between devices  34.2 us (7%)
  other arithmetic  33.9 us (6%)
  local copies, waits for them, and re-layouts  15.5 us (3%)
  between operations  14.2 us (3%)
    pallas_call x1, Pallas kernels, sum_rows(): pl.pallas_call(functools.partial(sum_kernel, count), out_shape=(block, bl...  162 us
    pallas_call x1, Pallas kernels, gather_rows(): pl.pallas_call(functools.partial(gather_kernel, count), out_shape=(full,...  143 us
    all_to_all x2, waiting for transfers between devices, spread(): lax.all_to_all(block.reshape(count, part, block.shape[1]), 'expert', spli...  39.7 us
    convert_element_type x2, other arithmetic, rows_by_gather(): rows_cot = (prob * rows_g.astype(jnp.float32)).astype(jnp.bfloat16)  16.2 us
    all_to_all x2, starting transfers between devices, spread(): lax.all_to_all(block.reshape(count, part, block.shape[1]), 'expert', spli...  13.4 us
    all_to_all x2, waiting for transfers between devices, land(): lax.all_to_all(ordered, 'expert', split_axis=0, concat_axis=0, tiled=True)  13 us
    dot_general x1, matrix products, expert_backward(): lax.dot_general(rows_cot, w_down, (((1,), (1,)), ((), ())), preferred_ele...  12.4 us
    all_to_all x2, starting transfers between devices, land(): lax.all_to_all(ordered, 'expert', split_axis=0, concat_axis=0, tiled=True)  12.3 us
  transfers between devices with their start and end apart: 7, of which 5 were waited for; matrix products, arithmetic and copies ran while one was open for 12% of the time, Pallas kernels for 58%

profile of v2, /device:TPU:0, one launch (start us, length us, event | category | flops | bytes accessed | tf_op | source)
XLA Modules:
  0.0 521.8 jit_solution(1835031993943953262)
XLA Ops:
  7.2 0.0 copy-start
  7.2 0.9 reduce_sum.39
  8.0 0.8 broadcast_divide_fusion
  8.8 0.8 select_reduce_fusion.1
  9.6 0.6 select_reduce_fusion
  10.2 8.3 %all-to-all-start = ((f32[16,1,128]{2,1,0:T(1,128)}), f32[16,1,128]{2,1,0:T(1,128)S(1)}, u32[]{:S(2)}, u32[]{:S(2)}) async-start(f32[16,1,128]{2,1,0:T(1,128)} %bitcast.2), calls=%async_computation | async-start | bytes 16384 | tf_op jit(solution)/shard_map/all_to_all | solution.py:317
  18.5 0.0 reduce-scatter.5.cloned.1.call-start
  18.6 143.1 %shard_map.147 = (bf16[16,128,2048]{2,1,0:T(8,128)(2,1)}, bf16[16,128,2048]{2,1,0:T(8,128)(2,1)}) custom-call(bf16[128,2048]{1,0:T(8,128)(2,1)} %refs_0_.1, bf16[128,2048]{1,0:T(8,128)(2,1)} %refs_1_.1), custom_call_target="tpu_custom_call" | custom-call | tf_op jit(solution)/shard_map/pallas_call | solution.py:175
  161.7 0.0 copy-done
  161.7 10.7 %fusion.9 = f32[2048,768]{0,1:T(8,128)} fusion(bf16[2048,2048]{1,0:T(8,128)(2,1)} %bitcast.65, bf16[1,2048,768]{2,1,0:T(8,128)(2,1)S(1)} %copy-done), kind=kOutput, calls=%fused_computation.19 | convolution fusion | flops 6442450944 | bytes 17825792 | tf_op jit(solution)/shard_map/dot_general | solution.py:21
  172.4 0.0 all-to-all-done
  172.4 8.0 %multiply_convert_fusion = bf16[16,128,2048]{2,1,0:T(8,128)(2,1)} fusion(f32[16,128]{1,0:T(8,128)S(1)} %bitcast.62, bf16[16,128,2048]{2,1,0:T(8,128)(2,1)} %get-tuple-element.9), kind=kLoop, calls=%fused_computation.4 | loop fusion | flops 12582912 | bytes 16785408 | tf_op jit(solution)/shard_map/convert_element_type | solution.py:321
  180.5 0.0 copy-start.3
  180.5 8.1 %fusion = bf16[2048,2048]{1,0:T(8,128)(2,1)} fusion(f32[2048]{0:T(1024)S(1)} %bitcast.63, bf16[16,128,2048]{2,1,0:T(8,128)(2,1)} %get-tuple-element.9), kind=kLoop, calls=%fused_computation.3 | loop fusion | flops 12582912 | bytes 16785408 | tf_op jit(solution)/shard_map/convert_element_type | solution.py:321
  188.6 0.0 copy-done.3
  188.6 0.0 copy-start.1
  188.6 12.4 %multiply_convert_fusion.3 = (bf16[2048,384]{0,1:T(8,128)(2,1)}, bf16[2048,384]{0,1:T(8,128)(2,1)}, bf16[2048,384]{0,1:T(8,128)(2,1)S(1)}) fusion(f32[2048,768]{0,1:T(8,128)} %fusion.9, bf16[2048,2048]{1,0:T(8,128)(2,1)} %bitcast.59, bf16[1,384,2048]{2,1,0:T(8,128)(2,1)S(1)} %copy-done.3), kind=kOutput, calls=%fused_computation.22 | convolution fusion | flops 3233808384 | bytes 20971520 | tf_op jit(solution)/shard_map/dot_general | solution.py:34
  201.0 0.0 copy-start.5
  201.0 1.1 copy-done.5
  202.2 0.0 copy-done.1
  202.2 4.6 convolution_convert_fusion.2
  206.7 0.0 reduce-scatter.5.cloned.1.call-update
  206.8 0.2 reduce-scatter.3.cloned.1.call-start
  207.0 11.3 %convolution_convert_fusion.1 = bf16[2048,768]{1,0:T(8,128)(2,1)} fusion(bf16[2048,2048]{1,0:T(8,128)(2,1)} %bitcast.66, bf16[2048,384]{0,1:T(8,128)(2,1)} %get-tuple-element.13, bf16[2048,384]{0,1:T(8,128)(2,1)} %get-tuple-element.12), kind=kOutput, calls=%fused_computation.9 | convolution fusion | flops 6450315264 | bytes 14680064 | tf_op jit(solution)/shard_map/dot_general | solution.py:43
  218.3 0.0 reduce-scatter.3.cloned.1.call-update
  218.3 6.0 %reduce-scatter.5.cloned.1.call-done = bf16[384,1024]{1,0:T(8,128)(2,1)} async-done(((bf16[384,2048]{1,0:T(8,128)(2,1)}), bf16[384,1024]{1,0:T(8,128)(2,1)}) %reduce-scatter.5.cloned.1.call-update) | async-done | bytes 786448 | tf_op jit(solution)/shard_map/reduce_scatter | solution.py:410
  224.3 3.7 fusion.22
  228.0 8.1 %all-to-all-start.3 = ((bf16[16,24,1024]{2,1,0:T(8,128)(2,1)}), bf16[16,24,1024]{2,1,0:T(8,128)(2,1)}, u32[]{:S(2)}, u32[]{:S(2)}) async-start(bf16[16,24,1024]{2,1,0:T(8,128)(2,1)} %bitcast.61), calls=%async_computation.5 | async-start | bytes 1572864 | tf_op jit(solution)/shard_map/all_to_all | solution.py:64
  236.0 2.8 reduce-scatter.3.cloned.1.call-done
  238.8 6.0 %fusion.11 = bf16[1024,768]{1,0:T(8,128)(2,1)} fusion(bf16[1,1024,768]{2,1,0:T(8,128)(2,1)} %param.21, bf16[1024,768]{1,0:T(8,128)(2,1)} %reduce-scatter.3.cloned.1.call-done, bf16[1,1024,768]{2,1,0:T(8,128)(2,1)} %param.20), kind=kLoop, calls=%fused_computation.25 | loop fusion | flops 11796480 | bytes 6291456 | tf_op jit(solution)/shard_map/convert_element_type | solution.py:57
  244.8 0.0 copy-start.2
  244.8 0.0 copy-start.4
  244.8 10.7 %all-to-all-done.3 = bf16[16,24,1024]{2,1,0:T(8,128)(2,1)} async-done(((bf16[16,24,1024]{2,1,0:T(8,128)(2,1)}), bf16[16,24,1024]{2,1,0:T(8,128)(2,1)}, u32[]{:S(2)}, u32[]{:S(2)}) %all-to-all-start.3) | async-done | bytes 786464 | tf_op jit(solution)/shard_map/all_to_all | solution.py:64
  255.4 5.3 %all-to-all-start.1 = ((bf16[16,64,768]{2,1,0:T(8,128)(2,1)}), bf16[16,64,768]{2,1,0:T(8,128)(2,1)}, u32[]{:S(2)}, u32[]{:S(2)}) async-start(bf16[16,64,768]{2,1,0:T(8,128)(2,1)} %bitcast.60), calls=%async_computation.2 | async-start | bytes 3145728 | tf_op jit(solution)/shard_map/all_to_all | solution.py:64
  260.8 0.0 copy-done.2
  260.8 0.0 copy-done.4
  260.8 0.1 select_reduce_fusion.2
  261.0 2.6 gather_fusion.1
  263.6 2.1 broadcast_select_fusion.1
  265.7 29.0 %all-to-all-done.1 = bf16[16,64,768]{2,1,0:T(8,128)(2,1)} async-done(((bf16[16,64,768]{2,1,0:T(8,128)(2,1)}), bf16[16,64,768]{2,1,0:T(8,128)(2,1)}, u32[]{:S(2)}, u32[]{:S(2)}) %all-to-all-start.1) | async-done | bytes 1572896 | tf_op jit(solution)/shard_map/all_to_all | solution.py:64
  294.7 7.3 %all-to-all-start.4 = ((bf16[16,24,1024]{2,1,0:T(8,128)(2,1)}), bf16[16,24,1024]{2,1,0:T(8,128)(2,1)}, u32[]{:S(2)}, u32[]{:S(2)}) async-start(bf16[16,24,1024]{2,1,0:T(8,128)(2,1)} %broadcast_select_fusion.1), calls=%async_computation.6 | async-start | bytes 1572864 | tf_op jit(solution)/shard_map/all_to_all | solution.py:71
  302.1 3.2 gather_fusion
  305.3 2.8 broadcast_select_fusion
  308.1 13.0 %all-to-all-done.4 = bf16[16,24,1024]{2,1,0:T(8,128)(2,1)} async-done(((bf16[16,24,1024]{2,1,0:T(8,128)(2,1)}), bf16[16,24,1024]{2,1,0:T(8,128)(2,1)}, u32[]{:S(2)}, u32[]{:S(2)}) %all-to-all-start.4) | async-done | bytes 786464 | tf_op jit(solution)/shard_map/all_to_all | solution.py:71
  321.1 4.9 all-to-all-start.2
  326.1 0.0 copy-start.6
  326.1 0.0 copy-start.7
  326.1 9.8 %multiply_convert_fusion.1 = bf16[2048,2048]{1,0:T(8,128)(2,1)} fusion(f32[2048]{0:T(1024)S(1)} %bitcast.64, bf16[2048,384]{0,1:T(8,128)(2,1)} %copy-done.5, bf16[1,384,2048]{2,1,0:T(8,128)(2,1)} %param.19), kind=kOutput, calls=%fused_computation.5 | convolution fusion | flops 3238002688 | bytes 11542528 | tf_op jit(solution)/shard_map/dot_general | solution.py:25
  335.9 0.0 copy-done.6
  335.9 0.0 copy-done.7
  335.9 9.0 %convolution_convert_fusion = bf16[2048,2048]{1,0:T(8,128)(2,1)} fusion(bf16[1,2048,768]{2,1,0:T(8,128)(2,1)S(1)} %copy-done, bf16[2048,384]{0,1:T(8,128)(2,1)S(1)} %copy-done.7, bf16[2048,384]{0,1:T(8,128)(2,1)S(1)} %copy-done.6), kind=kOutput, calls=%fused_computation.6 | convolution fusion | flops 6452936704 | bytes 14680064 | tf_op jit(solution)/shard_map/dot_general | solution.py:40
  344.9 161.5 %shard_map.148 = (bf16[128,2048]{1,0:T(8,128)(2,1)}, bf16[128,2048]{1,0:T(8,128)(2,1)}) custom-call(bf16[16,128,2048]{2,1,0:T(8,128)(2,1)} %bitcast.57, bf16[16,128,2048]{2,1,0:T(8,128)(2,1)} %bitcast.58), custom_call_target="tpu_custom_call" | custom-call | tf_op jit(solution)/shard_map/pallas_call | solution.py:288
  506.4 0.0 all-to-all-done.2
  506.4 1.9 copy.25
  508.3 1.9 copy.26
  510.2 2.7 copy.27
  512.9 2.1 copy.28
  (3 shorter events, 0.0 us)
Async XLA Ops:
  7.2 154.5 %copy-start = (bf16[1,2048,768]{2,1,0:T(8,128)(2,1)S(1)}, bf16[1,2048,768]{2,1,0:T(8,128)(2,1)}, u32[]{:S(2)}) copy-start(bf16[1,2048,768]{2,1,0:T(8,128)(2,1)} %param.18) | copy-start | bytes 9437188
  10.2 162.2 %all-to-all-start = ((f32[16,1,128]{2,1,0:T(1,128)}), f32[16,1,128]{2,1,0:T(1,128)S(1)}, u32[]{:S(2)}, u32[]{:S(2)}) async-start(f32[16,1,128]{2,1,0:T(1,128)} %bitcast.2), calls=%async_computation | async-start | bytes 16384 | tf_op jit(solution)/shard_map/all_to_all | solution.py:317
  18.5 205.8 %reduce-scatter.5.cloned.1.call-start = ((), (), s32[]{:S(2)}) async-start(), calls=%async_computation.8 | async-start | bytes 2359296 | tf_op jit(solution)/shard_map/reduce_scatter | solution.py:410
  180.5 8.2 %copy-start.3 = (bf16[1,384,2048]{2,1,0:T(8,128)(2,1)S(1)}, bf16[1,384,2048]{2,1,0:T(8,128)(2,1)}, u32[]{:S(2)}) copy-start(bf16[1,384,2048]{2,1,0:T(8,128)(2,1)} %param.19) | copy-start | bytes 4718596
  188.6 13.5 %copy-start.1 = (bf16[2048,2048]{1,0:T(8,128)(2,1)S(1)}, bf16[2048,2048]{1,0:T(8,128)(2,1)}, u32[]{:S(2)}) copy-start(bf16[2048,2048]{1,0:T(8,128)(2,1)} %fusion) | copy-start | bytes 25165828
  201.0 1.1 copy-start.5
  206.8 32.0 %reduce-scatter.3.cloned.1.call-start = ((), (), s32[]{:S(2)}) async-start(), calls=%async_computation.7 | async-start | bytes 4718592 | tf_op jit(solution)/shard_map/reduce_scatter | solution.py:407
  228.0 27.5 %all-to-all-start.3 = ((bf16[16,24,1024]{2,1,0:T(8,128)(2,1)}), bf16[16,24,1024]{2,1,0:T(8,128)(2,1)}, u32[]{:S(2)}, u32[]{:S(2)}) async-start(bf16[16,24,1024]{2,1,0:T(8,128)(2,1)} %bitcast.61), calls=%async_computation.5 | async-start | bytes 1572864 | tf_op jit(solution)/shard_map/all_to_all | solution.py:64
  244.8 16.0 %copy-start.2 = (s32[16]{0:T(128)S(1)}, s32[16]{0:T(128)}, u32[]{:S(2)}) copy-start(s32[16]{0:T(128)} %param.16) | copy-start | bytes 196
  244.8 16.0 %copy-start.4 = (s32[16]{0:T(128)S(1)}, s32[16]{0:T(128)}, u32[]{:S(2)}) copy-start(s32[16]{0:T(128)} %param.17) | copy-start | bytes 196
  255.4 39.3 %all-to-all-start.1 = ((bf16[16,64,768]{2,1,0:T(8,128)(2,1)}), bf16[16,64,768]{2,1,0:T(8,128)(2,1)}, u32[]{:S(2)}, u32[]{:S(2)}) async-start(bf16[16,64,768]{2,1,0:T(8,128)(2,1)} %bitcast.60), calls=%async_computation.2 | async-start | bytes 3145728 | tf_op jit(solution)/shard_map/all_to_all | solution.py:64
  294.7 26.4 %all-to-all-start.4 = ((bf16[16,24,1024]{2,1,0:T(8,128)(2,1)}), bf16[16,24,1024]{2,1,0:T(8,128)(2,1)}, u32[]{:S(2)}, u32[]{:S(2)}) async-start(bf16[16,24,1024]{2,1,0:T(8,128)(2,1)} %broadcast_select_fusion.1), calls=%async_computation.6 | async-start | bytes 1572864 | tf_op jit(solution)/shard_map/all_to_all | solution.py:71
  321.1 185.3 %all-to-all-start.2 = ((bf16[16,64,768]{2,1,0:T(8,128)(2,1)}), bf16[16,64,768]{2,1,0:T(8,128)(2,1)}, u32[]{:S(2)}, u32[]{:S(2)}) async-start(bf16[16,64,768]{2,1,0:T(8,128)(2,1)} %broadcast_select_fusion), calls=%async_computation.3 | async-start | bytes 3145728 | tf_op jit(solution)/shard_map/all_to_all | solution.py:71
  326.1 9.9 %copy-start.6 = (bf16[2048,384]{0,1:T(8,128)(2,1)S(1)}, bf16[2048,384]{0,1:T(8,128)(2,1)}, u32[]{:S(2)}) copy-start(bf16[2048,384]{0,1:T(8,128)(2,1)} %get-tuple-element.12) | copy-start | bytes 4718596
  326.1 9.8 %copy-start.7 = (bf16[2048,384]{0,1:T(8,128)(2,1)S(1)}, bf16[2048,384]{0,1:T(8,128)(2,1)}, u32[]{:S(2)}) copy-start(bf16[2048,384]{0,1:T(8,128)(2,1)} %get-tuple-element.13) | copy-start | bytes 4718596
Sparse Core Ops, SparseCore 0:
  206.9 17.3 reduce-scatter.4
  226.6 12.1 reduce-scatter.2

commit v3 on v2

--- a/solution.py
+++ b/solution.py
@@ -16,17 +16,20 @@
 epsilon = 1e-08
 
 
-def expert_forward(rows_x, w_gu, w_down):
-    hidden = w_down.shape[0]
+def expert_forward(rows_x, w_gu):
+    hidden = w_gu.shape[1] // 2
     both = jnp.dot(rows_x, w_gu, preferred_element_type=jnp.float32)
     gate = both[:, :hidden]
     upper = both[:, hidden:]
     activated = (gate * jax.nn.sigmoid(gate) * upper).astype(jnp.bfloat16)
-    output = jnp.dot(activated, w_down, preferred_element_type=jnp.float32).astype(jnp.bfloat16)
-    return (both, activated, output)
-
-
-def expert_backward(rows_x, rows_cot, both, activated, w_gu, w_down):
+    return (both, activated)
+
+
+def expert_output(activated, w_down):
+    return jnp.dot(activated, w_down, preferred_element_type=jnp.float32).astype(jnp.bfloat16)
+
+
+def expert_backward(rows_x, rows_cot, both, activated, w_down):
     hidden = w_down.shape[0]
     gate = both[:, :hidden]
     upper = both[:, hidden:]
@@ -37,16 +40,19 @@
     grad_gate = grad_act * upper * (sigmoid_gate * (1.0 + gate * (1.0 - sigmoid_gate)))
     grad_upper = grad_act * gate * sigmoid_gate
     grad_both = jnp.concatenate([grad_gate, grad_upper], axis=1).astype(jnp.bfloat16)
-    row_grad = lax.dot_general(
+    grad_gu = lax.dot_general(
+        rows_x, grad_both, (((0,), (0,)), ((), ())), preferred_element_type=jnp.float32
+    )
+    grad_down = lax.dot_general(
+        activated, rows_cot, (((0,), (0,)), ((), ())), preferred_element_type=jnp.float32
+    )
+    return (grad_both, grad_gu, grad_down)
+
+
+def expert_row_grad(grad_both, w_gu):
+    return lax.dot_general(
         grad_both, w_gu, (((1,), (1,)), ((), ())), preferred_element_type=jnp.float32
     ).astype(jnp.bfloat16)
-    grad_gu = lax.dot_general(
-        rows_x, grad_both, (((0,), (0,)), ((), ())), preferred_element_type=jnp.float32
-    )
-    grad_down = lax.dot_general(
-        activated, rows_cot, (((0,), (0,)), ((), ())), preferred_element_type=jnp.float32
-    )
-    return (row_grad, grad_gu, grad_down)
 
 
 def adam_direction(first, second, grad):
@@ -59,17 +65,27 @@
     )
 
 
-def spread(block, count):
-    part = block.shape[0] // count
-    return lax.all_to_all(
-        block.reshape(count, part, block.shape[1]), "expert", split_axis=0, concat_axis=0, tiled=True
-    )
-
-
-def land(pieces, source):
-    ordered = jnp.take(pieces, source, axis=0)
-    back = lax.all_to_all(ordered, "expert", split_axis=0, concat_axis=0, tiled=True)
-    return back.reshape(-1, back.shape[2])
+def pack(step_gu, step_down):
+    wide = step_gu.shape[1]
+    rest = step_down.shape[1] - wide
+    tail = step_down[:, wide:].reshape(wide // rest, -1, rest)
+    beside = jnp.concatenate([tail[i] for i in range(wide // rest)], axis=1)
+    return jnp.concatenate([step_gu, step_down[:, :wide], beside], axis=0)
+
+
+def unpack(rows, step_gu, step_down):
+    wide = step_gu.shape[1]
+    rest = step_down.shape[1] - wide
+    upper = step_gu.shape[0]
+    lower = upper + step_down.shape[0]
+    tail = jnp.concatenate(
+        [rows[lower:, i * rest : (i + 1) * rest] for i in range(wide // rest)], axis=0
+    )
+    return (rows[:upper], jnp.concatenate([rows[upper:lower], tail], axis=1))
+
+
+def exchange(pieces):
+    return lax.all_to_all(pieces, "expert", split_axis=0, concat_axis=0, tiled=True)
 
 
 def position(count):
@@ -193,15 +209,19 @@
 
 def sum_kernel(count, *refs):
     tensors = 2
-    parts, outs = refs[:tensors], refs[tensors : 2 * tensors]
+    parts, leaving = refs[:tensors], refs[tensors]
+    outs, landed = refs[tensors + 1 : 2 * tensors + 1], refs[2 * tensors + 1]
     (got_d, got_xy, got_z, out_xy, out_z,
-     z_send, z_recv, xy_send, xy_recv, d_send, d_recv) = refs[2 * tensors :]
+     z_send, z_recv, xy_send, xy_recv, d_send, d_recv,
+     leg_send, leg_recv, own_sem) = refs[2 * tensors + 2 :]
     deep, z, y, x = position(count)
     core = lax.axis_index("dp")
     half = outs[0].shape[0] // 2
     up = [(slot_of((z + k) % deep, y, x), core) for k in range(deep)]
     beside = ((slot_of(z, y, 1 - x), core), (slot_of(z, 1 - y, x), core))
-    greet(up[1:] + list(beside))
+    me = slot_of(z, y, x)
+    others = [lax.rem(me + j, count) for j in range(1, count)]
+    greet([(other, core) for other in others])
 
     def copy(src, dst, send, recv, device):
         return pltpu.make_async_remote_copy(
@@ -226,6 +246,15 @@
             step.start()
             first[t, k, way] = step
             sent.append(step)
+    own = pltpu.make_async_copy(leaving.at[me], landed.at[me], own_sem)
+    own.start()
+    legs = []
+    for j, other in enumerate(others):
+        step = copy(
+            leaving.at[other], landed.at[me], leg_send.at[j], leg_recv.at[j], (other, core)
+        )
+        step.start()
+        legs.append(step)
     second = {}
 
     def pass_on(t, k):
@@ -274,11 +303,18 @@
             third[t, k].wait_recv()
             total = total + wide(got_z, (t, k - 1))
         outs[t][...] = total.astype(jnp.bfloat16)
-    for step in sent:
+    for j, step in enumerate(legs):
+        origin = lax.rem(me + count - j - 1, count)
+        copy(
+            leaving.at[origin], landed.at[origin], leg_send.at[j], leg_recv.at[j],
+            (others[j], core),
+        ).wait_recv()
+    own.wait()
+    for step in sent + legs:
         step.wait_send()
 
 
-def sum_rows(part_out, part_grad):
+def sum_rows(part_out, part_grad, leaving):
     count = lax.axis_size("expert")
     rows, width = part_out.shape[0] // count, part_out.shape[1]
     deep = count // PLANE
@@ -287,9 +323,10 @@
     vmem = lambda *lead: pltpu.VMEM(lead + (width,), jnp.bfloat16)
     return pl.pallas_call(
         functools.partial(sum_kernel, count),
-        out_shape=(block, block),
-        in_specs=[pl.BlockSpec(memory_space=pltpu.VMEM)] * 2,
-        out_specs=(pl.BlockSpec(memory_space=pltpu.VMEM),) * 2,
+        out_shape=(block, block, jax.ShapeDtypeStruct(leaving.shape, leaving.dtype)),
+        in_specs=[pl.BlockSpec(memory_space=pltpu.VMEM)] * 2 + [pl.BlockSpec(memory_space=pl.ANY)],
+        out_specs=(pl.BlockSpec(memory_space=pltpu.VMEM),) * 2
+        + (pl.BlockSpec(memory_space=pl.ANY),),
         scratch_shapes=[
             vmem(2, deep, 2, rows // 2),
             vmem(2, deep, 2, rows),
@@ -302,14 +339,17 @@
             dma((2, deep, 2)),
             dma((2, deep, 2)),
             dma((2, deep, 2)),
+            dma((count - 1,)),
+            dma((count - 1,)),
+            dma,
         ],
         compiler_params=pltpu.CompilerParams(
             collective_id=1, has_side_effects=True, vmem_limit_bytes=56 * 1024 * 1024
         ),
-    )(part_out.reshape(count, rows, width), part_grad.reshape(count, rows, width))
-
-
-def rows_by_gather(tokens, out_grad, target, probs, w_gu, w_down):
+    )(part_out.reshape(count, rows, width), part_grad.reshape(count, rows, width), leaving)
+
+
+def rows_by_gather(tokens, out_grad, target, probs, w_gu, w_down, relocate):
     count = lax.axis_size("expert")
     lanes = jnp.arange(count, dtype=jnp.int32)
     chosen = target[:, :, None] == lanes[None, None, :]
@@ -317,16 +357,19 @@
     prob_in = lax.all_to_all(weights, "expert", split_axis=0, concat_axis=0, tiled=True)
     rows_x, rows_g = gather_rows(tokens, out_grad)
     prob = prob_in.reshape(-1, 1)
-    both, activated, output = expert_forward(rows_x, w_gu, w_down)
+    both, activated = expert_forward(rows_x, w_gu)
     rows_cot = (prob * rows_g.astype(jnp.float32)).astype(jnp.bfloat16)
-    row_grad, grad_gu, grad_down = expert_backward(rows_x, rows_cot, both, activated, w_gu, w_down)
-    mixed, token_grad = sum_rows(
-        (prob * output.astype(jnp.float32)).astype(jnp.bfloat16), row_grad
-    )
-    return (mixed, token_grad, grad_gu, grad_down)
-
-
-def rows_by_exchange(tokens, out_grad, target, probs, w_gu, w_down):
+    grad_both, grad_gu, grad_down = expert_backward(rows_x, rows_cot, both, activated, w_down)
+    step, pieces, ordered = relocate(grad_gu, grad_down)
+    activated, grad_both, _ = lax.optimization_barrier((activated, grad_both, step))
+    output = expert_output(activated, w_down)
+    part_out = (prob * output.astype(jnp.float32)).astype(jnp.bfloat16)
+    row_grad = expert_row_grad(grad_both, w_gu)
+    mixed, token_grad, landed = sum_rows(part_out, row_grad, ordered)
+    return (mixed, token_grad, landed)
+
+
+def rows_by_exchange(tokens, out_grad, target, probs, w_gu, w_down, relocate):
     count = lax.axis_size("expert")
     tok_rows, width = tokens.shape
     top = target.shape[1]
@@ -352,13 +395,15 @@
     )
     recv_x = lax.all_to_all(send_x, "expert", split_axis=0, concat_axis=0, tiled=True)
     rows_x = recv_x.reshape(rows, width)
-    both, activated, output = expert_forward(rows_x, w_gu, w_down)
+    both, activated = expert_forward(rows_x, w_gu)
+    output = expert_output(activated, w_down)
     back_out = lax.all_to_all(
         output.reshape(count, capacity, width), "expert", split_axis=0, concat_axis=0, tiled=True
     )
     recv_cot = lax.all_to_all(send_cot, "expert", split_axis=0, concat_axis=0, tiled=True)
     rows_cot = recv_cot.reshape(rows, width)
-    row_grad, grad_gu, grad_down = expert_backward(rows_x, rows_cot, both, activated, w_gu, w_down)
+    grad_both, grad_gu, grad_down = expert_backward(rows_x, rows_cot, both, activated, w_down)
+    row_grad = expert_row_grad(grad_both, w_gu)
     back_grad = lax.all_to_all(
         row_grad.reshape(count, capacity, width), "expert", split_axis=0, concat_axis=0, tiled=True
     )
@@ -372,7 +417,7 @@
     coarse = lax.reduce_precision(weight, 8, 7)
     mixed = (back_pick(coarse, back_out) + back_pick(weight - coarse, back_out)).astype(jnp.bfloat16)
     token_grad = back_pick(pick, back_grad).astype(jnp.bfloat16)
-    return (mixed, token_grad, grad_gu, grad_down)
+    return (mixed, token_grad, exchange(relocate(grad_gu, grad_down)[2]))
 
 
 def per_device(
@@ -400,22 +445,29 @@
     )
     gathered = count % (2 * PLANE) == 0 and 2 * expert_ids.shape[1] >= count
     rows_plan = rows_by_gather if gathered else rows_by_exchange
-    mixed, token_grad, grad_gu, grad_down = rows_plan(
-        tokens, out_grad, target, probs, gate_up[0], down[0]
-    )
-    share_gu, share_down = (
-        lax.psum_scatter(
-            grad_gu.astype(jnp.bfloat16), "dp", scatter_dimension=0, tiled=True
-        ).astype(jnp.float32),
-        lax.psum_scatter(
-            grad_down.astype(jnp.bfloat16), "dp", scatter_dimension=1, tiled=True
-        ).astype(jnp.float32),
-    )
-    step_gu = adam_direction(first_gu[0], second_gu[0], share_gu)
-    step_down = adam_direction(first_down[0], second_down[0], share_down)
-    update_gu = land(spread(step_gu, count), source)[None]
-    update_down = land(spread(step_down, count), source)[None]
-    return (mixed, token_grad, update_gu, update_down)
+
+    def relocate(grad_gu, grad_down):
+        share_gu, share_down = (
+            lax.psum_scatter(
+                grad_gu.astype(jnp.bfloat16), "dp", scatter_dimension=0, tiled=True
+            ).astype(jnp.float32),
+            lax.psum_scatter(
+                grad_down.astype(jnp.bfloat16), "dp", scatter_dimension=1, tiled=True
+            ).astype(jnp.float32),
+        )
+        step_gu = adam_direction(first_gu[0], second_gu[0], share_gu)
+        step_down = adam_direction(first_down[0], second_down[0], share_down)
+        step = pack(step_gu, step_down)
+        pieces = exchange(step.reshape(count, -1, step.shape[1]))
+        return (step, pieces, jnp.take(pieces, source, axis=0, mode="clip"))
+
+    mixed, token_grad, landed = rows_plan(
+        tokens, out_grad, target, probs, gate_up[0], down[0], relocate
+    )
+    update_gu, update_down = unpack(
+        landed.reshape(-1, landed.shape[2]), first_gu[0], first_down[0]
+    )
+    return (mixed, token_grad, update_gu[None], update_down[None])
 
 
 def solution(mesh):

time: 523 us -> 517 us (0.989)
  Pallas kernels: 305 us -> 334 us
  starting transfers between devices: 34.2 us -> 15.5 us
  waiting for transfers between devices: 61.5 us -> 45.7 us
    pallas_call x1, Pallas kernels: 162 us -> 191 us  [sum_rows(): pl.pallas_call(functools.partial(sum_kernel, count), out_shape=(block, bl...]
    all_to_all x4 -> x1, waiting for transfers between devices: 52.7 us -> 28.9 us  [exchange(): lax.all_to_all(pieces, 'expert', split_axis=0, concat_axis=0, tiled=True)]
    all_to_all x4 -> x1, starting transfers between devices: 25.7 us -> 6.93 us  [exchange(): lax.all_to_all(pieces, 'expert', split_axis=0, concat_axis=0, tiled=True)]
    concatenate x0 -> x2, other arithmetic: none -> 11 us  [the longest x1 8.58 us: pack(): return jnp.concatenate([step_gu, step_down[:, :wide], beside], axis=0)]
    reduce_scatter x2, waiting for transfers between devices: 8.76 us -> 16.8 us  [the longest x1 10.8 us: relocate(): lax.psum_scatter(grad_gu.astype(jnp.bfloat16), 'dp', scatter_dimension=0,...]
    unnamed x20 -> x24, local copies, waits for them, and re-layouts: 9.66 us -> 4.02 us
  transfers between devices with their start and end apart: 7 -> 4, of which waited for: 5 -> 3; matrix products, arithmetic and copies ran while one was open for 12% -> 8% of each run, Pallas kernels for 58% -> 28%
where the time goes in v3:
time: 517 us; the launch traced here: 516 us
  Pallas kernels  334 us (65%)
  matrix products  55.1 us (11%)
  waiting for transfers between devices  45.7 us (9%)
  other arithmetic  39 us (8%)
  starting transfers between devices  15.5 us (3%)
  between operations  14.2 us (3%)
  local copies, waits for them, and re-layouts  12.6 us (2%)
    pallas_call x1, Pallas kernels, sum_rows(): pl.pallas_call(functools.partial(sum_kernel, count), out_shape=(block, bl...  191 us
    pallas_call x1, Pallas kernels, gather_rows(): pl.pallas_call(functools.partial(gather_kernel, count), out_shape=(full,...  143 us
    all_to_all x1, waiting for transfers between devices, exchange(): lax.all_to_all(pieces, 'expert', split_axis=0, concat_axis=0, tiled=True)  28.9 us
    convert_element_type x2, other arithmetic, rows_by_gather(): rows_cot = (prob * rows_g.astype(jnp.float32)).astype(jnp.bfloat16)  16.2 us
    dot_general x1, matrix products, expert_backward(): lax.dot_general(rows_cot, w_down, (((1,), (1,)), ((), ())), preferred_ele...  12.4 us
    dot_general x1, matrix products, expert_backward(): lax.dot_general(rows_x, grad_both, (((0,), (0,)), ((), ())), preferred_el...  11.3 us
    dot_general x1, matrix products, expert_forward(): both = jnp.dot(rows_x, w_gu, preferred_element_type=jnp.float32)  11 us
    reduce_scatter x1, waiting for transfers between devices, relocate(): lax.psum_scatter(grad_gu.astype(jnp.bfloat16), 'dp', scatter_dimension=0,...  10.8 us
  transfers between devices with their start and end apart: 4, of which 3 were waited for; matrix products, arithmetic and copies ran while one was open for 8% of the time, Pallas kernels for 28%

profile of v3, /device:TPU:0, one launch (start us, length us, event | category | flops | bytes accessed | tf_op | source)
XLA Modules:
  0.0 516.4 jit_solution(1961770592997866545)
XLA Ops:
  7.2 0.0 copy-start
  7.2 0.9 reduce_sum.37
  8.0 0.8 broadcast_divide_fusion
  8.8 0.8 select_reduce_fusion.1
  9.6 0.6 select_reduce_fusion
  10.2 8.3 %all-to-all-start = ((f32[16,1,128]{2,1,0:T(1,128)}), f32[16,1,128]{2,1,0:T(1,128)S(1)}, u32[]{:S(2)}, u32[]{:S(2)}) async-start(f32[16,1,128]{2,1,0:T(1,128)} %bitcast.2), calls=%async_computation | async-start | bytes 16384 | tf_op jit(solution)/shard_map/all_to_all | solution.py:357
  18.5 0.0 reduce-scatter.5.cloned.1.call-start
  18.6 143.1 %shard_map.147 = (bf16[16,128,2048]{2,1,0:T(8,128)(2,1)}, bf16[16,128,2048]{2,1,0:T(8,128)(2,1)}) custom-call(bf16[128,2048]{1,0:T(8,128)(2,1)} %refs_0_.1, bf16[128,2048]{1,0:T(8,128)(2,1)} %refs_1_.1), custom_call_target="tpu_custom_call" | custom-call | tf_op jit(solution)/shard_map/pallas_call | solution.py:191
  161.7 0.0 copy-done
  161.7 11.0 %fusion.9 = f32[2048,768]{0,1:T(8,128)} fusion(bf16[2048,2048]{1,0:T(8,128)(2,1)} %bitcast.66, bf16[1,2048,768]{2,1,0:T(8,128)(2,1)S(1)} %copy-done), kind=kOutput, calls=%fused_computation.18 | convolution fusion | flops 6442450944 | bytes 17825792 | tf_op jit(solution)/shard_map/dot_general | solution.py:21
  172.7 0.0 all-to-all-done
  172.7 8.0 %multiply_convert_fusion.1 = bf16[16,128,2048]{2,1,0:T(8,128)(2,1)} fusion(f32[16,128]{1,0:T(8,128)S(1)} %bitcast.63, bf16[16,128,2048]{2,1,0:T(8,128)(2,1)} %get-tuple-element.12), kind=kLoop, calls=%fused_computation.4 | loop fusion | flops 12582912 | bytes 16785408 | tf_op jit(solution)/shard_map/convert_element_type | solution.py:361
  180.7 0.0 copy-start.6
  180.7 8.2 %fusion = bf16[2048,2048]{1,0:T(8,128)(2,1)} fusion(f32[2048]{0:T(1024)S(1)} %bitcast.64, bf16[16,128,2048]{2,1,0:T(8,128)(2,1)} %get-tuple-element.12), kind=kLoop, calls=%fused_computation.2 | loop fusion | flops 12582912 | bytes 16785408 | tf_op jit(solution)/shard_map/convert_element_type | solution.py:361
  188.9 0.0 copy-done.6
  188.9 0.0 copy-start.1
  188.9 12.4 %multiply_convert_fusion.3 = (bf16[2048,384]{0,1:T(8,128)(2,1)}, bf16[2048,384]{0,1:T(8,128)(2,1)}, bf16[2048,384]{0,1:T(8,128)(2,1)S(1)}) fusion(f32[2048,768]{0,1:T(8,128)} %fusion.9, bf16[2048,2048]{1,0:T(8,128)(2,1)} %bitcast.59, bf16[1,384,2048]{2,1,0:T(8,128)(2,1)S(1)} %copy-done.6), kind=kOutput, calls=%fused_computation.21 | convolution fusion | flops 3233808384 | bytes 20971520 | tf_op jit(solution)/shard_map/dot_general | solution.py:37
  201.3 0.0 copy-start.9
  201.3 1.2 copy-done.9
  202.4 0.0 copy-done.1
  202.4 4.6 convolution_convert_fusion.2
  207.0 0.0 reduce-scatter.5.cloned.1.call-update
  207.0 0.2 reduce-scatter.3.cloned.1.call-start
  207.3 11.3 %convolution_convert_fusion.1 = bf16[2048,768]{1,0:T(8,128)(2,1)} fusion(bf16[2048,2048]{1,0:T(8,128)(2,1)} %bitcast.67, bf16[2048,384]{0,1:T(8,128)(2,1)} %get-tuple-element.19, bf16[2048,384]{0,1:T(8,128)(2,1)} %get-tuple-element.18), kind=kOutput, calls=%fused_computation.8 | convolution fusion | flops 6450315264 | bytes 14680064 | tf_op jit(solution)/shard_map/dot_general | solution.py:43
  218.6 0.0 reduce-scatter.3.cloned.1.call-update
  218.6 6.0 %reduce-scatter.5.cloned.1.call-done = bf16[384,1024]{1,0:T(8,128)(2,1)} async-done(((bf16[384,2048]{1,0:T(8,128)(2,1)}), bf16[384,1024]{1,0:T(8,128)(2,1)}) %reduce-scatter.5.cloned.1.call-update) | async-done | bytes 786448 | tf_op jit(solution)/shard_map/reduce_scatter | solution.py:454
  224.6 2.8 fusion.22
  227.4 0.0 copy-start.2
  227.4 0.9 copy-done.2
  228.3 10.8 %reduce-scatter.3.cloned.1.call-done = bf16[1024,768]{1,0:T(8,128)(2,1)} async-done(((bf16[2048,768]{1,0:T(8,128)(2,1)}), bf16[1024,768]{1,0:T(8,128)(2,1)}) %reduce-scatter.3.cloned.1.call-update) | async-done | bytes 1572880 | tf_op jit(solution)/shard_map/reduce_scatter | solution.py:451
  239.1 0.0 slice-start
  239.1 4.9 fusion.11
  244.0 0.0 slice-done
  244.0 8.6 %maximum_maximum_fusion = bf16[1536,768]{1,0:T(8,128)(2,1)} fusion(bf16[128,256]{1,0:T(8,128)(2,1)S(1)} %get-tuple-element.25, bf16[128,256]{1,0:T(8,128)(2,1)S(1)} %get-tuple-element.26, bf16[128,256]{1,0:T(8,128)(2,1)S(1)} %get-tuple-element.24, bf16[384,768]{1,0:T(8,128)(2,1)S(1)} %slice-done, bf16[1024,768]{1,0:T(8,128)(2,1)S(1)} %fusion.11), kind=kLoop, calls=%fused_computation.27 | loop fusion | flops 11796480 | bytes 4718592 | tf_op jit(solution)/shard_map/concatenate | solution.py:73
  252.6 0.0 copy-start.5
  252.6 0.0 copy-start.8
  252.6 6.9 %all-to-all-start.1 = ((bf16[16,96,768]{2,1,0:T(8,128)(2,1)}), bf16[16,96,768]{2,1,0:T(8,128)(2,1)}, u32[]{:S(2)}, u32[]{:S(2)}) async-start(bf16[16,96,768]{2,1,0:T(8,128)(2,1)} %bitcast.56), calls=%async_computation.3 | async-start | bytes 4718592 | tf_op jit(solution)/shard_map/all_to_all | solution.py:88
  259.5 0.0 copy-done.5
  259.5 0.0 copy-done.8
  259.5 0.1 select_reduce_fusion.2
  259.6 0.0 copy-start.7
  259.6 0.0 copy-start.10
  259.7 2.4 pad_maximum_fusion
  262.1 0.0 copy-done.7
  262.1 0.4 copy-done.10
  262.5 6.8 %multiply_convert_fusion = bf16[2048,2048]{1,0:T(8,128)(2,1)} fusion(f32[2048]{0:T(1024)S(1)} %bitcast.65, bf16[2048,384]{0,1:T(8,128)(2,1)S(1)} %copy-done.10, bf16[1,384,2048]{2,1,0:T(8,128)(2,1)S(1)} %copy-done.7), kind=kOutput, calls=%fused_computation.3 | convolution fusion | flops 3238002688 | bytes 11542528 | tf_op jit(solution)/shard_map/dot_general | solution.py:29
  269.3 9.0 %convolution_convert_fusion = bf16[2048,2048]{1,0:T(8,128)(2,1)} fusion(bf16[2048,768]{0,1:T(8,128)(2,1)S(1)} %pad_maximum_fusion, bf16[1,2048,768]{2,1,0:T(8,128)(2,1)S(1)} %copy-done), kind=kOutput, calls=%fused_computation.5 | convolution fusion | flops 6446645248 | bytes 14680064 | tf_op jit(solution)/shard_map/dot_general | solution.py:53
  278.2 28.9 %all-to-all-done.1 = bf16[16,96,768]{2,1,0:T(8,128)(2,1)} async-done(((bf16[16,96,768]{2,1,0:T(8,128)(2,1)}), bf16[16,96,768]{2,1,0:T(8,128)(2,1)}, u32[]{:S(2)}, u32[]{:S(2)}) %all-to-all-start.1) | async-done | bytes 2359328 | tf_op jit(solution)/shard_map/all_to_all | solution.py:88
  307.2 3.8 gather_fusion
  310.9 191.3 %shard_map.148 = (bf16[128,2048]{1,0:T(8,128)(2,1)}, bf16[128,2048]{1,0:T(8,128)(2,1)}, bf16[16,96,768]{2,1,0:T(8,128)(2,1)}) custom-call(bf16[16,128,2048]{2,1,0:T(8,128)(2,1)} %bitcast.57, bf16[16,128,2048]{2,1,0:T(8,128)(2,1)} %bitcast.58, bf16[16,96,768]{2,1,0:T(8,128)(2,1)} %gather_fusion), custom_call_target="tpu_custom_call" | custom-call | tf_op jit(solution)/shard_map/pallas_call | solution.py:324
  502.2 0.0 copy-start.4
  502.2 1.2 slice.62
  503.4 0.0 copy-start.3
  503.4 1.0 fusion.23
  504.4 2.7 slice_bitcast_fusion
  507.0 1.0 maximum_bitcast_fusion
  508.0 0.0 copy-done.4
  508.0 0.8 copy.23
  508.8 0.0 copy-done.3
  508.8 0.8 copy.24
  (2 shorter events, 0.0 us)
Async XLA Ops:
  7.2 154.5 %copy-start = (bf16[1,2048,768]{2,1,0:T(8,128)(2,1)S(1)}, bf16[1,2048,768]{2,1,0:T(8,128)(2,1)}, u32[]{:S(2)}) copy-start(bf16[1,2048,768]{2,1,0:T(8,128)(2,1)} %param.18) | copy-start | bytes 9437188
  10.2 162.5 %all-to-all-start = ((f32[16,1,128]{2,1,0:T(1,128)}), f32[16,1,128]{2,1,0:T(1,128)S(1)}, u32[]{:S(2)}, u32[]{:S(2)}) async-start(f32[16,1,128]{2,1,0:T(1,128)} %bitcast.2), calls=%async_computation | async-start | bytes 16384 | tf_op jit(solution)/shard_map/all_to_all | solution.py:357
  18.5 206.1 %reduce-scatter.5.cloned.1.call-start = ((), (), s32[]{:S(2)}) async-start(), calls=%async_computation.5 | async-start | bytes 2359296 | tf_op jit(solution)/shard_map/reduce_scatter | solution.py:454
  180.7 8.2 %copy-start.6 = (bf16[1,384,2048]{2,1,0:T(8,128)(2,1)S(1)}, bf16[1,384,2048]{2,1,0:T(8,128)(2,1)}, u32[]{:S(2)}) copy-start(bf16[1,384,2048]{2,1,0:T(8,128)(2,1)} %param.19) | copy-start | bytes 4718596
  188.9 13.5 %copy-start.1 = (bf16[2048,2048]{1,0:T(8,128)(2,1)S(1)}, bf16[2048,2048]{1,0:T(8,128)(2,1)}, u32[]{:S(2)}) copy-start(bf16[2048,2048]{1,0:T(8,128)(2,1)} %fusion) | copy-start | bytes 25165828
  201.3 1.2 copy-start.9
  207.0 32.0 %reduce-scatter.3.cloned.1.call-start = ((), (), s32[]{:S(2)}) async-start(), calls=%async_computation.4 | async-start | bytes 4718592 | tf_op jit(solution)/shard_map/reduce_scatter | solution.py:451
  227.4 0.9 copy-start.2
  239.1 4.9 slice-start
  252.6 6.9 %copy-start.5 = (s32[16]{0:T(128)S(1)}, s32[16]{0:T(128)}, u32[]{:S(2)}) copy-start(s32[16]{0:T(128)} %param.16) | copy-start | bytes 196
  252.6 6.9 %copy-start.8 = (s32[16]{0:T(128)S(1)}, s32[16]{0:T(128)}, u32[]{:S(2)}) copy-start(s32[16]{0:T(128)} %param.17) | copy-start | bytes 196
  252.6 54.6 %all-to-all-start.1 = ((bf16[16,96,768]{2,1,0:T(8,128)(2,1)}), bf16[16,96,768]{2,1,0:T(8,128)(2,1)}, u32[]{:S(2)}, u32[]{:S(2)}) async-start(bf16[16,96,768]{2,1,0:T(8,128)(2,1)} %bitcast.56), calls=%async_computation.3 | async-start | bytes 4718592 | tf_op jit(solution)/shard_map/all_to_all | solution.py:88
  259.6 2.5 copy-start.7
  259.6 2.8 copy-start.10
  502.2 5.8 %copy-start.4 = (bf16[128,2048]{1,0:T(8,128)(2,1)S(1)}, bf16[128,2048]{1,0:T(8,128)(2,1)}, u32[]{:S(2)}) copy-start(bf16[128,2048]{1,0:T(8,128)(2,1)} %get-tuple-element.31) | copy-start | bytes 1572868
  503.4 5.4 %copy-start.3 = (bf16[128,2048]{1,0:T(8,128)(2,1)S(1)}, bf16[128,2048]{1,0:T(8,128)(2,1)}, u32[]{:S(2)}) copy-start(bf16[128,2048]{1,0:T(8,128)(2,1)} %get-tuple-element.32) | copy-start | bytes 1572868
Sparse Core Ops, SparseCore 0:
  207.2 17.4 reduce-scatter.4
  227.0 12.0 reduce-scatter.2

commit v4 on v3

--- a/solution.py
+++ b/solution.py
@@ -358,7 +358,7 @@
     rows_x, rows_g = gather_rows(tokens, out_grad)
     prob = prob_in.reshape(-1, 1)
     both, activated = expert_forward(rows_x, w_gu)
-    rows_cot = (prob * rows_g.astype(jnp.float32)).astype(jnp.bfloat16)
+    rows_cot = lax.optimization_barrier((prob * rows_g.astype(jnp.float32)).astype(jnp.bfloat16))
     grad_both, grad_gu, grad_down = expert_backward(rows_x, rows_cot, both, activated, w_down)
     step, pieces, ordered = relocate(grad_gu, grad_down)
     activated, grad_both, _ = lax.optimization_barrier((activated, grad_both, step))

time: 517 us -> 509 us (0.985)
  other arithmetic: 39 us -> 31 us
    convert_element_type x2 -> x1, other arithmetic: 16.2 us -> 8.16 us  [rows_by_gather(): (prob * rows_g.astype(jnp.float32)).astype(jnp.bfloat16)]
  transfers between devices with their start and end apart: 4 -> 4, of which waited for: 3 -> 3; matrix products, arithmetic and copies ran while one was open for 8% -> 9% of each run, Pallas kernels for 28% -> 28%
where the time goes in v4:
time: 509 us; the launch traced here: 508 us
  Pallas kernels  334 us (66%)
  matrix products  55 us (11%)
  waiting for transfers between devices  45.7 us (9%)
  other arithmetic  31 us (6%)
  starting transfers between devices  15.5 us (3%)
  between operations  14.2 us (3%)
  local copies, waits for them, and re-layouts  12.6 us (2%)
    pallas_call x1, Pallas kernels, sum_rows(): pl.pallas_call(functools.partial(sum_kernel, count), out_shape=(block, bl...  191 us
    pallas_call x1, Pallas kernels, gather_rows(): pl.pallas_call(functools.partial(gather_kernel, count), out_shape=(full,...  143 us
    all_to_all x1, waiting for transfers between devices, exchange(): lax.all_to_all(pieces, 'expert', split_axis=0, concat_axis=0, tiled=True)  28.9 us
    dot_general x1, matrix products, expert_backward(): lax.dot_general(rows_cot, w_down, (((1,), (1,)), ((), ())), preferred_ele...  12.4 us
    dot_general x1, matrix products, expert_backward(): lax.dot_general(rows_x, grad_both, (((0,), (0,)), ((), ())), preferred_el...  11.3 us
    dot_general x1, matrix products, expert_forward(): both = jnp.dot(rows_x, w_gu, preferred_element_type=jnp.float32)  10.9 us
    reduce_scatter x1, waiting for transfers between devices, relocate(): lax.psum_scatter(grad_gu.astype(jnp.bfloat16), 'dp', scatter_dimension=0,...  10.8 us
  transfers between devices with their start and end apart: 4, of which 3 were waited for; matrix products, arithmetic and copies ran while one was open for 9% of the time, Pallas kernels for 28%

profile of v4, /device:TPU:0, one launch (start us, length us, event | category | flops | bytes accessed | tf_op | source)
XLA Modules:
  0.0 508.3 jit_solution(14888894502372429631)
XLA Ops:
  7.2 0.0 copy-start
  7.2 0.9 reduce_sum.37
  8.0 0.8 broadcast_divide_fusion
  8.8 0.8 select_reduce_fusion.1
  9.6 0.6 select_reduce_fusion
  10.2 8.3 %all-to-all-start = ((f32[16,1,128]{2,1,0:T(1,128)}), f32[16,1,128]{2,1,0:T(1,128)S(1)}, u32[]{:S(2)}, u32[]{:S(2)}) async-start(f32[16,1,128]{2,1,0:T(1,128)} %bitcast.2), calls=%async_computation | async-start | bytes 16384 | tf_op jit(solution)/shard_map/all_to_all | solution.py:357
  18.5 0.0 reduce-scatter.5.cloned.1.call-start
  18.6 143.1 %shard_map.147 = (bf16[16,128,2048]{2,1,0:T(8,128)(2,1)}, bf16[16,128,2048]{2,1,0:T(8,128)(2,1)}) custom-call(bf16[128,2048]{1,0:T(8,128)(2,1)} %refs_0_.1, bf16[128,2048]{1,0:T(8,128)(2,1)} %refs_1_.1), custom_call_target="tpu_custom_call" | custom-call | tf_op jit(solution)/shard_map/pallas_call | solution.py:191
  161.7 0.0 copy-done
  161.7 10.9 %fusion.9 = f32[2048,768]{0,1:T(8,128)} fusion(bf16[2048,2048]{1,0:T(8,128)(2,1)} %bitcast.61, bf16[1,2048,768]{2,1,0:T(8,128)(2,1)S(1)} %copy-done), kind=kOutput, calls=%fused_computation.17 | convolution fusion | flops 6442450944 | bytes 17825792 | tf_op jit(solution)/shard_map/dot_general | solution.py:21
  172.6 0.0 all-to-all-done
  172.6 0.0 copy-start.6
  172.6 8.2 %fusion = bf16[2048,2048]{1,0:T(8,128)(2,1)} fusion(bf16[16,128,2048]{2,1,0:T(8,128)(2,1)} %get-tuple-element.12, f32[2048]{0:T(1024)S(1)} %bitcast.59), kind=kLoop, calls=%fused_computation.2 | loop fusion | flops 12582912 | bytes 16785408 | tf_op jit(solution)/shard_map/convert_element_type | solution.py:361
  180.7 0.0 copy-done.6
  180.7 0.0 copy-start.1
  180.8 12.4 %multiply_convert_fusion.2 = (bf16[2048,384]{0,1:T(8,128)(2,1)}, bf16[2048,384]{0,1:T(8,128)(2,1)}, bf16[2048,384]{0,1:T(8,128)(2,1)S(1)}) fusion(f32[2048,768]{0,1:T(8,128)} %fusion.9, bf16[2048,2048]{1,0:T(8,128)(2,1)} %fusion, bf16[1,384,2048]{2,1,0:T(8,128)(2,1)S(1)} %copy-done.6), kind=kOutput, calls=%fused_computation.20 | convolution fusion | flops 3233808384 | bytes 20971520 | tf_op jit(solution)/shard_map/dot_general | solution.py:37
  193.1 0.0 copy-start.9
  193.1 1.2 copy-done.9
  194.3 0.0 copy-done.1
  194.3 4.6 convolution_convert_fusion.2
  198.9 0.0 reduce-scatter.5.cloned.1.call-update
  198.9 0.2 reduce-scatter.3.cloned.1.call-start
  199.2 11.3 %convolution_convert_fusion.1 = bf16[2048,768]{1,0:T(8,128)(2,1)} fusion(bf16[2048,2048]{1,0:T(8,128)(2,1)} %bitcast.62, bf16[2048,384]{0,1:T(8,128)(2,1)} %get-tuple-element.19, bf16[2048,384]{0,1:T(8,128)(2,1)} %get-tuple-element.18), kind=kOutput, calls=%fused_computation.7 | convolution fusion | flops 6450315264 | bytes 14680064 | tf_op jit(solution)/shard_map/dot_general | solution.py:43
  210.5 0.0 reduce-scatter.3.cloned.1.call-update
  210.5 6.0 %reduce-scatter.5.cloned.1.call-done = bf16[384,1024]{1,0:T(8,128)(2,1)} async-done(((bf16[384,2048]{1,0:T(8,128)(2,1)}), bf16[384,1024]{1,0:T(8,128)(2,1)}) %reduce-scatter.5.cloned.1.call-update) | async-done | bytes 786448 | tf_op jit(solution)/shard_map/reduce_scatter | solution.py:454
  216.5 2.8 fusion.22
  219.3 0.0 copy-start.2
  219.3 0.9 copy-done.2
  220.2 10.8 %reduce-scatter.3.cloned.1.call-done = bf16[1024,768]{1,0:T(8,128)(2,1)} async-done(((bf16[2048,768]{1,0:T(8,128)(2,1)}), bf16[1024,768]{1,0:T(8,128)(2,1)}) %reduce-scatter.3.cloned.1.call-update) | async-done | bytes 1572880 | tf_op jit(solution)/shard_map/reduce_scatter | solution.py:451
  231.0 0.0 slice-start
  231.0 4.9 fusion.11
  235.8 0.0 slice-done
  235.9 8.6 %maximum_maximum_fusion = bf16[1536,768]{1,0:T(8,128)(2,1)} fusion(bf16[128,256]{1,0:T(8,128)(2,1)S(1)} %get-tuple-element.25, bf16[128,256]{1,0:T(8,128)(2,1)S(1)} %get-tuple-element.26, bf16[128,256]{1,0:T(8,128)(2,1)S(1)} %get-tuple-element.24, bf16[384,768]{1,0:T(8,128)(2,1)S(1)} %slice-done, bf16[1024,768]{1,0:T(8,128)(2,1)S(1)} %fusion.11), kind=kLoop, calls=%fused_computation.26 | loop fusion | flops 11796480 | bytes 4718592 | tf_op jit(solution)/shard_map/concatenate | solution.py:73
  244.4 0.0 copy-start.5
  244.4 0.0 copy-start.8
  244.4 6.9 %all-to-all-start.1 = ((bf16[16,96,768]{2,1,0:T(8,128)(2,1)}), bf16[16,96,768]{2,1,0:T(8,128)(2,1)}, u32[]{:S(2)}, u32[]{:S(2)}) async-start(bf16[16,96,768]{2,1,0:T(8,128)(2,1)} %bitcast.53), calls=%async_computation.3 | async-start | bytes 4718592 | tf_op jit(solution)/shard_map/all_to_all | solution.py:88
  251.4 0.0 copy-done.5
  251.4 0.0 copy-done.8
  251.4 0.1 select_reduce_fusion.2
  251.5 0.0 copy-start.7
  251.5 0.0 copy-start.10
  251.5 2.4 pad_maximum_fusion
  254.0 0.0 copy-done.7
  254.0 0.4 copy-done.10
  254.4 6.8 %multiply_convert_fusion = bf16[2048,2048]{1,0:T(8,128)(2,1)} fusion(f32[2048]{0:T(1024)S(1)} %bitcast.60, bf16[2048,384]{0,1:T(8,128)(2,1)S(1)} %copy-done.10, bf16[1,384,2048]{2,1,0:T(8,128)(2,1)S(1)} %copy-done.7), kind=kOutput, calls=%fused_computation.3 | convolution fusion | flops 3238002688 | bytes 11542528 | tf_op jit(solution)/shard_map/dot_general | solution.py:29
  261.1 9.0 %convolution_convert_fusion = bf16[2048,2048]{1,0:T(8,128)(2,1)} fusion(bf16[2048,768]{0,1:T(8,128)(2,1)S(1)} %pad_maximum_fusion, bf16[1,2048,768]{2,1,0:T(8,128)(2,1)S(1)} %copy-done), kind=kOutput, calls=%fused_computation.4 | convolution fusion | flops 6446645248 | bytes 14680064 | tf_op jit(solution)/shard_map/dot_general | solution.py:53
  270.1 28.9 %all-to-all-done.1 = bf16[16,96,768]{2,1,0:T(8,128)(2,1)} async-done(((bf16[16,96,768]{2,1,0:T(8,128)(2,1)}), bf16[16,96,768]{2,1,0:T(8,128)(2,1)}, u32[]{:S(2)}, u32[]{:S(2)}) %all-to-all-start.1) | async-done | bytes 2359328 | tf_op jit(solution)/shard_map/all_to_all | solution.py:88
  299.1 3.8 gather_fusion
  302.8 191.3 %shard_map.148 = (bf16[128,2048]{1,0:T(8,128)(2,1)}, bf16[128,2048]{1,0:T(8,128)(2,1)}, bf16[16,96,768]{2,1,0:T(8,128)(2,1)}) custom-call(bf16[16,128,2048]{2,1,0:T(8,128)(2,1)} %bitcast.54, bf16[16,128,2048]{2,1,0:T(8,128)(2,1)} %bitcast.55, bf16[16,96,768]{2,1,0:T(8,128)(2,1)} %gather_fusion), custom_call_target="tpu_custom_call" | custom-call | tf_op jit(solution)/shard_map/pallas_call | solution.py:324
  494.1 0.0 copy-start.4
  494.1 1.2 slice.62
  495.3 0.0 copy-start.3
  495.3 1.0 fusion.23
  496.3 2.7 slice_bitcast_fusion
  498.9 1.0 maximum_bitcast_fusion
  499.9 0.0 copy-done.4
  499.9 0.8 copy.25
  500.7 0.0 copy-done.3
  500.7 0.8 copy.26
  (2 shorter events, 0.0 us)
Async XLA Ops:
  7.2 154.5 %copy-start = (bf16[1,2048,768]{2,1,0:T(8,128)(2,1)S(1)}, bf16[1,2048,768]{2,1,0:T(8,128)(2,1)}, u32[]{:S(2)}) copy-start(bf16[1,2048,768]{2,1,0:T(8,128)(2,1)} %param.18) | copy-start | bytes 9437188
  10.2 162.4 %all-to-all-start = ((f32[16,1,128]{2,1,0:T(1,128)}), f32[16,1,128]{2,1,0:T(1,128)S(1)}, u32[]{:S(2)}, u32[]{:S(2)}) async-start(f32[16,1,128]{2,1,0:T(1,128)} %bitcast.2), calls=%async_computation | async-start | bytes 16384 | tf_op jit(solution)/shard_map/all_to_all | solution.py:357
  18.5 197.9 %reduce-scatter.5.cloned.1.call-start = ((), (), s32[]{:S(2)}) async-start(), calls=%async_computation.5 | async-start | bytes 2359296 | tf_op jit(solution)/shard_map/reduce_scatter | solution.py:454
  172.6 8.2 %copy-start.6 = (bf16[1,384,2048]{2,1,0:T(8,128)(2,1)S(1)}, bf16[1,384,2048]{2,1,0:T(8,128)(2,1)}, u32[]{:S(2)}) copy-start(bf16[1,384,2048]{2,1,0:T(8,128)(2,1)} %param.19) | copy-start | bytes 4718596
  180.7 13.5 %copy-start.1 = (bf16[2048,2048]{1,0:T(8,128)(2,1)S(1)}, bf16[2048,2048]{1,0:T(8,128)(2,1)}, u32[]{:S(2)}) copy-start(bf16[2048,2048]{1,0:T(8,128)(2,1)} %fusion) | copy-start | bytes 25165828
  193.1 1.2 copy-start.9
  198.9 32.0 %reduce-scatter.3.cloned.1.call-start = ((), (), s32[]{:S(2)}) async-start(), calls=%async_computation.4 | async-start | bytes 4718592 | tf_op jit(solution)/shard_map/reduce_scatter | solution.py:451
  219.3 0.9 copy-start.2
  231.0 4.9 slice-start
  244.4 6.9 %copy-start.5 = (s32[16]{0:T(128)S(1)}, s32[16]{0:T(128)}, u32[]{:S(2)}) copy-start(s32[16]{0:T(128)} %param.16) | copy-start | bytes 196
  244.4 7.0 %copy-start.8 = (s32[16]{0:T(128)S(1)}, s32[16]{0:T(128)}, u32[]{:S(2)}) copy-start(s32[16]{0:T(128)} %param.17) | copy-start | bytes 196
  244.4 54.6 %all-to-all-start.1 = ((bf16[16,96,768]{2,1,0:T(8,128)(2,1)}), bf16[16,96,768]{2,1,0:T(8,128)(2,1)}, u32[]{:S(2)}, u32[]{:S(2)}) async-start(bf16[16,96,768]{2,1,0:T(8,128)(2,1)} %bitcast.53), calls=%async_computation.3 | async-start | bytes 4718592 | tf_op jit(solution)/shard_map/all_to_all | solution.py:88
  251.5 2.5 copy-start.7
  251.5 2.8 copy-start.10
  494.1 5.8 %copy-start.4 = (bf16[128,2048]{1,0:T(8,128)(2,1)S(1)}, bf16[128,2048]{1,0:T(8,128)(2,1)}, u32[]{:S(2)}) copy-start(bf16[128,2048]{1,0:T(8,128)(2,1)} %get-tuple-element.31) | copy-start | bytes 1572868
  495.3 5.4 %copy-start.3 = (bf16[128,2048]{1,0:T(8,128)(2,1)S(1)}, bf16[128,2048]{1,0:T(8,128)(2,1)}, u32[]{:S(2)}) copy-start(bf16[128,2048]{1,0:T(8,128)(2,1)} %get-tuple-element.32) | copy-start | bytes 1572868
Sparse Core Ops, SparseCore 0:
  199.0 17.3 reduce-scatter.4
  218.8 12.1 reduce-scatter.2
